TPU v7x, 512 devices: a whole 4x8x8 slice. The times are simulated.
512 devices in a mesh: seg: 8 (over y), dev: 64 (over z, x, core).
Axes of the slice: x: 4, y: 8, z: 8, core: 2. Of those that a mesh axis runs over, the one named last changes fastest.
Arguments:
- pressure: float32 [1024, 32768], P('seg', 'dev'), may hold values from -6 to 6
- pressure_prev: float32 [1024, 32768], P('seg', 'dev'), may hold values from -6 to 6
- permeability: float32 [1024, 32768], P('seg', 'dev'), may hold values from 0.1 to 2
- u_plus: float32 [4096, 3, 128], P(('seg', 'dev')), may hold values from -6 to 6
- u_minus: bfloat16 [4096, 3, 128], P(('seg', 'dev')), may hold values from -6 to 6
- node_state: int32 [4096, 128], P(('seg', 'dev')), may hold values from 0 to 2
- node_cell: int32 [4096, 128], P(('seg', 'dev')), may hold values from 0 to 65535
- pair_source: int32 [32768], P(('seg', 'dev')), may hold values from 0 to 7
- pair_dest: int32 [32768, 1], P(('seg', 'dev')), may hold values from 0 to 63; in each aligned block of 64 rows (0 to 63, 64 to 127, ...) at most 4 rows name the same one
- pair_target: int32 [32768], P(('seg', 'dev')), may hold values from 0 to 7
- mortar: bfloat16 [32768, 128, 128], P(('seg', 'dev')), may hold values from -0.5 to 0.5
Outputs:
- flow_residual: float32 [1024, 32768], P('seg', 'dev')
- traction_plus: float32 [4096, 3, 128], P(('seg', 'dev'))
- force_minus: float32 [4096, 3, 128], P(('seg', 'dev'))
Inputs may be any that keep to these rules, and one draw needn't show every extreme that they name: `pair_dest`: of the 64 pairs held by one device at most 4 name the same destination, and in every draw some device has exactly 4 pairs to one destination.
All inputs are finite; a program needn't handle non-finite values.
Results may differ from a plain program's by a relative error of at most 0.0025.
Values may be sent and summed in bfloat16 or wider, within the bound.
A program may use at most 64 MiB of HBM per device.

v0:
```python
import jax
import jax.numpy as jnp
from jax import lax
from jax.sharding import PartitionSpec as P

CAP = 4


COMPRESS = 0.5
PENALTY = 1.5
FRICTION = 0.6
CONFINING = 1.0


def extended(value, sides, width):
    for axis, dim in sides:
        count, length = (lax.axis_size(axis), value.shape[dim])
        up = [(i, (i + 1) % count) for i in range(count - 1)]
        down = [(j, i) for i, j in up]
        last = lax.slice_in_dim(value, length - width, length, axis=dim)
        initial = lax.slice_in_dim(value, 0, width, axis=dim)
        before = lax.ppermute(last, axis, up)
        after = lax.ppermute(initial, axis, down)
        value = jnp.concatenate([before, value, after], axis=dim)
    return value


def contact_law(jump, node_state, node_pressure):
    normal_part = PENALTY * jump[:, 0]
    tangent = jump[:, 1:]
    stress = CONFINING - node_pressure - normal_part
    limit_stress = FRICTION * jax.nn.softplus(stress)
    factor = limit_stress / jnp.sqrt(jnp.sum(tangent * tangent, axis=1) + 1.0)
    sliding = jnp.concatenate([normal_part[:, None], tangent * factor[:, None]], axis=1)
    state_wide = node_state[:, None, :]
    return jnp.where(
        state_wide == 0, PENALTY * jump, jnp.where(state_wide == 1, sliding, jnp.zeros_like(jump))
    )


def cell_residual(padded, pressure, permeability, pressure_prev):
    total = COMPRESS * (pressure - pressure_prev)
    for rows_cut, cols_cut in (
        (slice(2, None), slice(1, -1)),
        (slice(0, -2), slice(1, -1)),
        (slice(1, -1), slice(2, None)),
        (slice(1, -1), slice(0, -2)),
    ):
        neighbor_p = padded[0, rows_cut, cols_cut]
        neighbor_k = padded[1, rows_cut, cols_cut]
        conduct = 2.0 * permeability * neighbor_k / (permeability + neighbor_k)
        total = total + conduct * (pressure - neighbor_p)
    return total


def on_device(
    pressure,
    pressure_prev,
    permeability,
    u_plus,
    u_minus,
    node_state,
    node_cell,
    pair_source,
    pair_dest,
    pair_target,
    mortar,
):
    stacked = jnp.stack([pressure, permeability])
    padded = extended(stacked, (("seg", 1), ("dev", 2)), 1)
    flow_residual = cell_residual(padded, pressure, permeability, pressure_prev)
    peer_count = lax.axis_size("dev")
    slot_count = peer_count * CAP
    patch_count = u_plus.shape[0]
    node_count = u_plus.shape[2]
    destination = pair_dest[:, 0]
    dest_hit = (destination[:, None] == jnp.arange(peer_count, dtype=jnp.int32)[None, :]).astype(
        jnp.int32
    )
    slot_rank = jnp.sum(dest_hit * (jnp.cumsum(dest_hit, axis=0) - dest_hit), axis=1)
    pair_slot = destination * CAP + slot_rank
    placing = jnp.arange(slot_count, dtype=jnp.int32)[:, None] == pair_slot[None, :]
    minus_rows = u_minus[pair_source]
    projected = jnp.einsum("pij,pcj->pci", mortar, minus_rows, preferred_element_type=jnp.float32)
    outgoing = jnp.einsum(
        "sp,pcn->scn", placing.astype(jnp.float32), projected, precision=lax.Precision.HIGHEST
    )
    filled = jnp.any(placing, axis=1)
    target_slots = jnp.sum(jnp.where(placing, pair_target[None, :], 0), axis=1) + jnp.where(
        filled, 0, patch_count
    )
    incoming, incoming_target = (
        lax.all_to_all(
            outgoing.reshape(peer_count, CAP, 3, node_count),
            "dev",
            split_axis=0,
            concat_axis=0,
            tiled=True,
        ),
        lax.all_to_all(
            target_slots.reshape(peer_count, CAP), "dev", split_axis=0, concat_axis=0, tiled=True
        ),
    )
    incoming = incoming.reshape(slot_count, 3, node_count)
    owner_hit = (
        jnp.arange(patch_count, dtype=jnp.int32)[:, None] == incoming_target.reshape(-1)[None, :]
    ).astype(jnp.float32)
    mortar_sum = jnp.einsum("as,scn->acn", owner_hit, incoming, precision=lax.Precision.HIGHEST)
    jump = u_plus - mortar_sum
    node_pressure = pressure.reshape(-1)[node_cell]
    traction_plus = contact_law(jump, node_state, node_pressure)
    traction_half = traction_plus.astype(jnp.bfloat16)
    reply_slots = jnp.einsum(
        "as,acn->scn",
        owner_hit.astype(jnp.bfloat16),
        traction_half,
        preferred_element_type=jnp.float32,
    ).astype(jnp.bfloat16)
    returned = lax.all_to_all(
        reply_slots.reshape(peer_count, CAP, 3, node_count),
        "dev",
        split_axis=0,
        concat_axis=0,
        tiled=True,
    )
    pair_traction = returned.reshape(slot_count, 3, node_count)[pair_slot]
    reaction = jnp.einsum("pij,pci->pcj", mortar, pair_traction, preferred_element_type=jnp.float32)
    source_hit = (jnp.arange(patch_count, dtype=jnp.int32)[:, None] == pair_source[None, :]).astype(
        jnp.float32
    )
    force_minus = -jnp.einsum("bp,pcn->bcn", source_hit, reaction, precision=lax.Precision.HIGHEST)
    return (flow_residual, traction_plus, force_minus)


def solution(mesh):
    placed = (
        P("seg", "dev"),
        P("seg", "dev"),
        P("seg", "dev"),
        P(("seg", "dev"), None, None),
        P(("seg", "dev"), None, None),
        P(("seg", "dev"), None),
        P(("seg", "dev"), None),
        P(("seg", "dev")),
        P(("seg", "dev"), None),
        P(("seg", "dev")),
        P(("seg", "dev"), None, None),
    )
    return jax.shard_map(
        on_device,
        mesh=mesh,
        in_specs=placed,
        out_specs=(P("seg", "dev"), P(("seg", "dev"), None, None), P(("seg", "dev"), None, None)),
        check_vma=False,
    )
```

profile of v0, /device:TPU:1, one launch (start us, length us, event | category | flops | bytes accessed | tf_op | source)
XLA Modules:
  0.0 82.8 jit_solution(14270325375852431170)
XLA Ops:
  0.6 0.9 %fusion.27 = s32[64,64]{1,0:T(8,128)S(1)} fusion(s32[64]{0:T(128)} %bitcast.111), kind=kLoop, calls=%fused_computation.58 | loop fusion | flops 8192 | bytes 16640 | tf_op jit(solution)/shard_map/convert_element_type | solution.py:77
  1.6 0.8 %select_reduce_fusion.1 = s32[64]{0:T(128)S(1)} fusion(s32[64,64]{1,0:T(8,128)S(1)} %reduce_window_sum.11, s32[64]{0:T(128)} %bitcast.112), kind=kLoop, calls=%fused_computation.56 | loop fusion | flops 20416 | bytes 16896 | tf_op jit(solution)/shard_map/reduce_sum | solution.py:80
  2.5 0.7 multiply_add_fusion
  3.2 0.8 select_reduce_fusion
  4.0 0.7 add.93
  4.7 14.8 %all-to-all-start = ((s32[64,1,4]{2,1,0:T(1,128)}), s32[64,1,4]{2,1,0:T(1,128)S(1)}, u32[]{:S(2)}, u32[]{:S(2)}) async-start(s32[64,1,4]{2,1,0:T(1,128)} %bitcast.11), calls=%async_computation | async-start | bytes 65536 | tf_op jit(solution)/shard_map/all_to_all | solution.py:100
  19.6 0.8 pad_maximum_fusion.16
  20.3 1.3 %collective-permute-start = (f32[2,1,512]{2,1,0:T(1,128)S(1)}, f32[2,1,512]{2,1,0:T(1,128)S(1)}, u32[]{:S(2)}, u32[]{:S(2)}) collective-permute-start(f32[2,1,512]{2,1,0:T(1,128)S(1)} %get-tuple-element.6), channel_id=1, source_target_pairs={{64,0},{128,64},{192,128},{256,192},{320,256},{384,320},{448,384},... | collective-permute-start | bytes 12296 | tf_op jit(solution)/shard_map/ppermute | solution.py:23
  21.6 4.0 %collective-permute-start.1 = (f32[2,1,512]{2,1,0:T(1,128)S(1)}, f32[2,1,512]{2,1,0:T(1,128)S(1)}, u32[]{:S(2)}, u32[]{:S(2)}) collective-permute-start(f32[2,1,512]{2,1,0:T(1,128)S(1)} %get-tuple-element.5), channel_id=1, source_target_pairs={{0,64},{64,128},{128,192},{192,256},{256,320},{320,384},{384,448},... | collective-permute-start | bytes 12296 | tf_op jit(solution)/shard_map/ppermute | solution.py:22
  26.3 1.5 %gather_fusion = bf16[64,3,128]{2,0,1:T(8,128)(2,1)S(1)} fusion(bf16[8,3,128]{2,0,1:T(8,128)(2,1)} %param.15, s32[1024]{0:T(1024)S(1)} %pad_clamp_fusion.1), kind=kCustom, calls=%fused_computation | custom fusion | bytes 98560 | tf_op jit(solution)/shard_map/gather | solution.py:83
  27.8 1.2 %fusion.21 = f32[64,3,128]{2,1,0:T(4,128)S(1)} fusion(bf16[64,128,128]{2,1,0:T(8,128)(2,1)S(1)} %copy-done, bf16[64,3,128]{2,0,1:T(8,128)(2,1)S(1)} %gather_fusion), kind=kOutput, calls=%fused_computation.49 | convolution fusion | flops 6291456 | bytes 2244608 | tf_op jit(solution)/shard_map/pij,pcj->pci/dot_general | solution.py:84
  29.5 0.8 copy.18
  30.3 10.9 %all-to-all-start.1 = ((f32[64,4,3,128]{3,1,2,0:T(4,128)}), f32[64,4,3,128]{3,1,2,0:T(4,128)S(1)}, u32[]{:S(2)}, u32[]{:S(2)}) async-start(f32[64,4,3,128]{3,1,2,0:T(4,128)} %copy.18), calls=%async_computation.1 | async-start | bytes 786432 | tf_op jit(solution)/shard_map/all_to_all | solution.py:93
  41.3 6.2 %gather_fusion.1 = f32[1024]{0:T(1024)S(1)} fusion(f32[65536]{0:T(1024)S(1)} %bitcast.99, s32[1024]{0:T(1024)S(1)} %fusion.35), kind=kCustom, calls=%fused_computation.1 | custom fusion | bytes 12288 | tf_op jit(solution)/shard_map/gather | solution.py:110
  48.0 0.7 reduce.3
  48.9 0.8 pad_maximum_fusion.15
  49.7 2.4 %collective-permute-start.2 = (f32[2,130,1]{2,1,0:T(8,128)}, f32[2,130,1]{2,1,0:T(8,128)}, u32[]{:S(2)}, u32[]{:S(2)}) collective-permute-start(f32[2,130,1]{2,1,0:T(8,128)} %get-tuple-element.3), channel_id=1, source_target_pairs={{1,0},{2,1},{3,2},{4,3},{5,4},{6,5},{7,6},{8,7},{9,8},{10,9},{11,1... | collective-permute-start | bytes 3128 | tf_op jit(solution)/shard_map/ppermute | solution.py:23
  52.0 3.2 %collective-permute-start.3 = (f32[2,130,1]{2,1,0:T(8,128)}, f32[2,130,1]{2,1,0:T(8,128)}, u32[]{:S(2)}, u32[]{:S(2)}) collective-permute-start(f32[2,130,1]{2,1,0:T(8,128)} %get-tuple-element.4), channel_id=1, source_target_pairs={{0,1},{1,2},{2,3},{3,4},{4,5},{5,6},{6,7},{7,8},{8,9},{9,10},{10,1... | collective-permute-start | bytes 3128 | tf_op jit(solution)/shard_map/ppermute | solution.py:22
  55.2 1.1 %all-to-all-done.1 = f32[64,4,3,128]{3,1,2,0:T(4,128)S(1)} async-done(((f32[64,4,3,128]{3,1,2,0:T(4,128)}), f32[64,4,3,128]{3,1,2,0:T(4,128)S(1)}, u32[]{:S(2)}, u32[]{:S(2)}) %all-to-all-start.1) | async-done | bytes 393248 | tf_op jit(solution)/shard_map/all_to_all | solution.py:93
  57.0 0.7 copy.20
  57.7 10.8 %all-to-all-start.2 = ((bf16[64,4,3,128]{3,1,2,0:T(4,128)(2,1)}), bf16[64,4,3,128]{3,1,2,0:T(4,128)(2,1)S(1)}, u32[]{:S(2)}, u32[]{:S(2)}) async-start(bf16[64,4,3,128]{3,1,2,0:T(4,128)(2,1)} %copy.20), calls=%async_computation.2 | async-start | bytes 393216 | tf_op jit(solution)/shard_map/all_to_all | solution.py:119
  68.6 2.2 %fusion.3 = f32[128,512]{1,0:T(8,128)} fusion(f32[128,512]{1,0:T(8,128)S(1)} %copy-done.1, f32[2,130,1]{2,1,0:T(8,128)} %collective-permute-done.3, f32[2,1,512]{2,1,0:T(1,128)S(1)} %collective-permute-done, f32[2,1,512]{2,1,0:T(1,128)S(1)} %collective-permute-done.1, f32[1,128,512]{2,1,0:T(8,128)S(1)} %bitcast.106, f32[1,128,512]{2,1,0:T(8,128)S(1)} %bitcast.103, ...), kind=kLoop, calls=%fused_computation.10 | loop fusion | flops 3342336 | bytes 1583136 | tf_op jit(solution)/shard_map/add | solution.py:52
  70.8 9.8 %all-to-all-done.2 = bf16[64,4,3,128]{3,1,2,0:T(4,128)(2,1)S(1)} async-done(((bf16[64,4,3,128]{3,1,2,0:T(4,128)(2,1)}), bf16[64,4,3,128]{3,1,2,0:T(4,128)(2,1)S(1)}, u32[]{:S(2)}, u32[]{:S(2)}) %all-to-all-start.2) | async-done | bytes 196640 | tf_op jit(solution)/shard_map/all_to_all | solution.py:119
  82.0 0.8 convolution_negate_fusion
  (48 shorter events, 4.1 us)
Async XLA Ops:
  0.6 27.1 %copy-start = (bf16[64,128,128]{2,1,0:T(8,128)(2,1)S(1)}, bf16[64,128,128]{2,1,0:T(8,128)(2,1)}, u32[]{:S(2)}) copy-start(bf16[64,128,128]{2,1,0:T(8,128)(2,1)} %param.21) | copy-start | bytes 6291460
  4.7 25.6 %all-to-all-start = ((s32[64,1,4]{2,1,0:T(1,128)}), s32[64,1,4]{2,1,0:T(1,128)S(1)}, u32[]{:S(2)}, u32[]{:S(2)}) async-start(s32[64,1,4]{2,1,0:T(1,128)} %bitcast.11), calls=%async_computation | async-start | bytes 65536 | tf_op jit(solution)/shard_map/all_to_all | solution.py:100
  20.3 28.5 %collective-permute-start = (f32[2,1,512]{2,1,0:T(1,128)S(1)}, f32[2,1,512]{2,1,0:T(1,128)S(1)}, u32[]{:S(2)}, u32[]{:S(2)}) collective-permute-start(f32[2,1,512]{2,1,0:T(1,128)S(1)} %get-tuple-element.6), channel_id=1, source_target_pairs={{64,0},{128,64},{192,128},{256,192},{320,256},{384,320},{448,384},... | collective-permute-start | bytes 12296 | tf_op jit(solution)/shard_map/ppermute | solution.py:23
  21.6 27.2 %collective-permute-start.1 = (f32[2,1,512]{2,1,0:T(1,128)S(1)}, f32[2,1,512]{2,1,0:T(1,128)S(1)}, u32[]{:S(2)}, u32[]{:S(2)}) collective-permute-start(f32[2,1,512]{2,1,0:T(1,128)S(1)} %get-tuple-element.5), channel_id=1, source_target_pairs={{0,64},{64,128},{128,192},{192,256},{256,320},{320,384},{384,448},... | collective-permute-start | bytes 12296 | tf_op jit(solution)/shard_map/ppermute | solution.py:22
  27.8 13.4 %copy-start.6 = (s32[8,128]{1,0:T(8,128)S(1)}, s32[8,128]{1,0:T(8,128)}, u32[]{:S(2)}) copy-start(s32[8,128]{1,0:T(8,128)} %param.16) | copy-start | bytes 12292
  27.8 13.4 %copy-start.7 = (s32[8,128]{1,0:T(8,128)S(1)}, s32[8,128]{1,0:T(8,128)}, u32[]{:S(2)}) copy-start(s32[8,128]{1,0:T(8,128)} %param.17) | copy-start | bytes 12292
  27.8 13.4 %copy-start.8 = (s32[64,1]{0,1:T(1,128)S(1)}, s32[64,1]{0,1:T(1,128)}, u32[]{:S(2)}) copy-start(s32[64,1]{0,1:T(1,128)} %param.19) | copy-start | bytes 772
  27.8 13.4 %copy-start.1 = (f32[128,512]{1,0:T(8,128)S(1)}, f32[128,512]{1,0:T(8,128)}, u32[]{:S(2)}) copy-start(f32[128,512]{1,0:T(8,128)} %param.11) | copy-start | bytes 786436
  30.3 26.0 %all-to-all-start.1 = ((f32[64,4,3,128]{3,1,2,0:T(4,128)}), f32[64,4,3,128]{3,1,2,0:T(4,128)S(1)}, u32[]{:S(2)}, u32[]{:S(2)}) async-start(f32[64,4,3,128]{3,1,2,0:T(4,128)} %copy.18), calls=%async_computation.1 | async-start | bytes 786432 | tf_op jit(solution)/shard_map/all_to_all | solution.py:93
  41.3 7.6 %copy-start.2 = (f32[128,512]{1,0:T(8,128)S(1)}, f32[128,512]{1,0:T(8,128)}, u32[]{:S(2)}) copy-start(f32[128,512]{1,0:T(8,128)} %param.13) | copy-start | bytes 786436
  41.3 15.1 %copy-start.5 = (f32[8,3,128]{2,0,1:T(8,128)S(1)}, f32[8,3,128]{2,0,1:T(8,128)}, u32[]{:S(2)}) copy-start(f32[8,3,128]{2,0,1:T(8,128)} %param.14) | copy-start | bytes 36868
  47.5 21.1 %copy-start.3 = (f32[128,512]{1,0:T(8,128)S(1)}, f32[128,512]{1,0:T(8,128)}, u32[]{:S(2)}) copy-start(f32[128,512]{1,0:T(8,128)} %param.12) | copy-start | bytes 786436
  49.7 18.9 %collective-permute-start.2 = (f32[2,130,1]{2,1,0:T(8,128)}, f32[2,130,1]{2,1,0:T(8,128)}, u32[]{:S(2)}, u32[]{:S(2)}) collective-permute-start(f32[2,130,1]{2,1,0:T(8,128)} %get-tuple-element.3), channel_id=1, source_target_pairs={{1,0},{2,1},{3,2},{4,3},{5,4},{6,5},{7,6},{8,7},{9,8},{10,9},{11,1... | collective-permute-start | bytes 3128 | tf_op jit(solution)/shard_map/ppermute | solution.py:23
  52.0 16.6 %collective-permute-start.3 = (f32[2,130,1]{2,1,0:T(8,128)}, f32[2,130,1]{2,1,0:T(8,128)}, u32[]{:S(2)}, u32[]{:S(2)}) collective-permute-start(f32[2,130,1]{2,1,0:T(8,128)} %get-tuple-element.4), channel_id=1, source_target_pairs={{0,1},{1,2},{2,3},{3,4},{4,5},{5,6},{6,7},{7,8},{8,9},{9,10},{10,1... | collective-permute-start | bytes 3128 | tf_op jit(solution)/shard_map/ppermute | solution.py:22
  56.7 25.3 %copy-start.4 = (f32[8,3,128]{2,0,1:T(8,128)}, f32[8,3,128]{2,0,1:T(8,128)S(1)}, u32[]{:S(2)}) copy-start(f32[8,3,128]{2,0,1:T(8,128)S(1)} %fusion.28) | copy-start | bytes 36868
  57.7 22.8 %all-to-all-start.2 = ((bf16[64,4,3,128]{3,1,2,0:T(4,128)(2,1)}), bf16[64,4,3,128]{3,1,2,0:T(4,128)(2,1)S(1)}, u32[]{:S(2)}, u32[]{:S(2)}) async-start(bf16[64,4,3,128]{3,1,2,0:T(4,128)(2,1)} %copy.20), calls=%async_computation.2 | async-start | bytes 393216 | tf_op jit(solution)/shard_map/all_to_all | solution.py:119
  68.6 13.4 %copy-start.9 = (s32[64]{0:T(128)S(1)}, s32[64]{0:T(128)}, u32[]{:S(2)}) copy-start(s32[64]{0:T(128)} %param.18) | copy-start | bytes 772
where the time goes:
time: 83.8 us; the launch traced here: 82.8 us
  starting transfers between devices  47.3 us (56%)
  local copies, waits for them, and re-layouts  11.5 us (14%)
  waiting for transfers between devices  10.9 us (13%)
  other arithmetic  8.51 us (10%)
  matrix products  3.55 us (4%)
  between operations  0.98 us (1%)
    all_to_all x1, starting transfers between devices, on_device(): lax.all_to_all(target_slots.reshape(peer_count, CAP), 'dev', split_axis=0...  14.8 us
    all_to_all x1, starting transfers between devices, on_device(): lax.all_to_all(outgoing.reshape(peer_count, CAP, 3, node_count), 'dev', s...  10.9 us
    all_to_all x1, starting transfers between devices, on_device(): lax.all_to_all(reply_slots.reshape(peer_count, CAP, 3, node_count), 'dev'...  10.8 us
    all_to_all x1, waiting for transfers between devices, on_device(): lax.all_to_all(reply_slots.reshape(peer_count, CAP, 3, node_count), 'dev'...  9.81 us
    ppermute x2, starting transfers between devices, extended(): before = lax.ppermute(last, axis, up)  7.19 us
    gather x1, local copies, waits for them, and re-layouts, on_device(): node_pressure = pressure.reshape(-1)[node_cell]  6.15 us
    ppermute x2, starting transfers between devices, extended(): after = lax.ppermute(initial, axis, down)  3.63 us
    add x1, other arithmetic, cell_residual(): total = total + conduct * (pressure - neighbor_p)  2.16 us
  transfers between devices with their start and end apart: 7, of which 2 were waited for; matrix products, arithmetic and copies ran while one was open for 21% of the time, Pallas kernels for 0%

commit v1 on v0

v1 whole, which is shorter than its diff:
```python
import jax
import jax.numpy as jnp
from jax import lax
from jax.experimental import pallas as pl
from jax.experimental.pallas import tpu as pltpu
from jax.sharding import PartitionSpec as P

CAP = 4
COMPRESS = 0.5
PENALTY = 1.5
FRICTION = 0.6
CONFINING = 1.0

NX = 8
NP = 8
F32 = jnp.float32
BF16 = jnp.bfloat16
I32 = jnp.int32
MESH = pl.DeviceIdType.MESH


def iota(shape, dim):
    return lax.broadcasted_iota(I32, shape, dim)


def split3(value):
    high = value.astype(BF16)
    rest = value - high.astype(F32)
    mid = rest.astype(BF16)
    low = (rest - mid.astype(F32)).astype(BF16)
    return high, mid, low


def dot_nn(a, b):
    return lax.dot_general(a, b, (((1,), (0,)), ((), ())), preferred_element_type=F32)


def dot_nt(a, b):
    return lax.dot_general(a, b, (((1,), (1,)), ((), ())), preferred_element_type=F32)


def dot_tn(a, b):
    return lax.dot_general(a, b, (((0,), (0,)), ((), ())), preferred_element_type=F32)


def remote(src, dst, send, recv, device):
    return pltpu.make_async_remote_copy(
        src_ref=src, dst_ref=dst, send_sem=send, recv_sem=recv, device_id=device, device_id_type=MESH
    )


def exchange_kernel(
    pressure_h, prev_h, perm_h, uplus_r, uminus_r, state_r, cell_r, dest_r, target_r, source_s, mortar_h,
    pair_traction_o, traction_o, flow_o,
    pres, prev, perm, mort, flow, proj, slots_t, owner, zsend, zrecv, csend, crecv, xsend, xrecv,
    tsend, trecv, rsend, rrecv, row_send, row_recv, col_send, col_recv, node_p,
    msem, lsem, zss, zrs, css, crs, xss, xrs, tss, trs, rss, rrs, hss, hrs, osem,
):
    seg = lax.axis_index("seg")
    me = lax.axis_index("dev")
    n_seg = lax.axis_size("seg")
    n_dev = lax.axis_size("dev")
    x = lax.rem(me // 2, NX)
    pos = (me // (2 * NX)) * 2 + lax.rem(me, 2)

    def column(p):
        return {"dev": (p // 2) * (2 * NX) + x * 2 + lax.rem(p, 2)}

    def row(xx):
        return {"dev": (pos // 2) * (2 * NX) + xx * 2 + lax.rem(pos, 2)}

    seg_up, seg_down = {"seg": lax.rem(seg + 1, n_seg)}, {"seg": lax.rem(seg + n_seg - 1, n_seg)}
    dev_up, dev_down = {"dev": lax.rem(me + 1, n_dev)}, {"dev": lax.rem(me + n_dev - 1, n_dev)}

    mcopies = [
        pltpu.make_async_copy(mortar_h.at[pl.ds(8 * g, 8)], mort.at[pl.ds(8 * g, 8)], msem.at[g])
        for g in range(8)
    ]
    for copy in mcopies:
        copy.start()
    lcopies = [
        pltpu.make_async_copy(a, b, lsem.at[i])
        for i, (a, b) in enumerate(((pressure_h, pres), (perm_h, perm), (prev_h, prev)))
    ]
    for copy in lcopies:
        copy.start()

    barrier = pltpu.get_barrier_semaphore()
    for i in range(1, NP):
        pl.semaphore_signal(barrier, inc=1, device_id=column(lax.rem(pos + i, NP)), device_id_type=MESH)
    for i in range(1, NX):
        pl.semaphore_signal(barrier, inc=1, device_id=row(lax.rem(x + i, NX)), device_id_type=MESH)
    for device in (seg_up, seg_down, dev_up, dev_down):
        pl.semaphore_signal(barrier, inc=1, device_id=device, device_id_type=MESH)

    lane, sub = iota((64, 128), 1), iota((64, 128), 0)
    diagonal = lane == sub

    def as_column(ref):
        wide = jnp.concatenate([ref[...].reshape(1, 64), jnp.full((1, 64), -1, I32)], axis=1)
        wide = jnp.broadcast_to(wide, (64, 128))
        return wide, jnp.sum(jnp.where(diagonal, wide, 0), axis=1, keepdims=True)

    dest_row, dest = as_column(dest_r)
    _, target = as_column(target_r)
    rank = jnp.sum(jnp.where((dest_row == dest) & (lane < sub), 1, 0), axis=1, keepdims=True)
    slot = (((dest >> 4) * 2 + (dest & 1)) * NX + ((dest >> 1) & (NX - 1))) * CAP + rank
    for h in range(2):
        slots_t[:, 128 * h : 128 * (h + 1)] = jnp.where(slot == lane + 128 * h, 1.0, 0.0).astype(BF16)
    for p in range(NP):
        code = jnp.sum(jnp.where(slot == (lane & 31) + 32 * p, target, 0), axis=0, keepdims=True)
        csend[p] = jnp.broadcast_to(code.astype(F32), (8, 128))

    for g in range(8):
        mcopies[g].wait()

        def project(j, carry):
            q = 8 * g + j
            value = dot_nt(uminus_r[source_s[q]], mort[q])
            for c in range(3):
                proj[pl.ds(q, 1), 128 * c : 128 * (c + 1)] = value[c : c + 1, :]
            return carry

        lax.fori_loop(0, 8, project, 0, unroll=True)
    parts = split3(proj[...])
    hit = slots_t[...]
    placed = dot_tn(hit, parts[0]) + dot_tn(hit, parts[1]) + dot_tn(hit, parts[2])
    zsend[...] = placed.reshape(NP, 32, 384)

    pl.semaphore_wait(barrier, NP - 1 + NX - 1 + 4)

    zcopies, ccopies = [], []
    for i in range(1, NP):
        p = lax.rem(pos + i, NP)
        ccopies.append(remote(csend.at[p], crecv.at[pos], css.at[i], crs.at[pos], column(p)))
        zcopies.append(remote(zsend.at[p], zrecv.at[pos], zss.at[i], zrs.at[pos], column(p)))
        ccopies[-1].start()
        zcopies[-1].start()
    crecv[pos] = csend[pos]
    zrecv[pos] = zsend[pos]

    for copy in lcopies:
        copy.wait()
    for b in range(4):
        cut = slice(128 * b, 128 * (b + 1))
        row_send[0, b : b + 1, :] = pres[0:1, cut]
        row_send[0, 4 + b : 5 + b, :] = perm[0:1, cut]
        row_send[1, b : b + 1, :] = pres[127:128, cut]
        row_send[1, 4 + b : 5 + b, :] = perm[127:128, cut]
    lane2 = iota((128, 128), 1)
    edge = jnp.where(
        lane2 == 0,
        pres[:, 0:128],
        jnp.where(
            lane2 == 1,
            pltpu.roll(perm[:, 0:128], 1, 1),
            jnp.where(lane2 == 127, pres[:, 384:512], pltpu.roll(perm[:, 384:512], 127, 1)),
        ),
    )
    edge = edge.T
    col_send[0] = edge[0:8, :]
    col_send[1] = edge[120:128, :]
    hcopies = [
        remote(row_send.at[0], row_recv.at[1], hss.at[0], hrs.at[0], seg_down),
        remote(row_send.at[1], row_recv.at[0], hss.at[1], hrs.at[1], seg_up),
        remote(col_send.at[0], col_recv.at[1], hss.at[2], hrs.at[2], dev_down),
        remote(col_send.at[1], col_recv.at[0], hss.at[3], hrs.at[3], dev_up),
    ]
    for copy in hcopies:
        copy.start()

    cell = cell_r[...]
    cell_lane, cell_block = cell & 127, cell >> 7

    def look(r, found):
        lines = pres[pl.ds(pl.multiple_of(8 * r, 8), 8), :]
        for i in range(8):
            for b in range(4):
                line = jnp.broadcast_to(lines[i : i + 1, 128 * b : 128 * (b + 1)], (8, 128))
                picked = jnp.take_along_axis(line, cell_lane, axis=1)
                found = jnp.where(cell_block == 32 * r + (4 * i + b), picked, found)
        return found

    node_p[...] = lax.fori_loop(0, 16, look, jnp.zeros((8, 128), F32))

    for i in range(1, NP):
        p = lax.rem(pos + i, NP)
        remote(csend.at[p], crecv.at[p], css.at[i], crs.at[p], column(p)).wait_recv()
        remote(zsend.at[p], zrecv.at[p], zss.at[i], zrs.at[p], column(p)).wait_recv()
    for h in range(2):
        code = jnp.zeros((8, 128), F32)
        for p in range(4):
            code = jnp.where((iota((8, 128), 1) >> 5) == p, crecv[4 * h + p], code)
        code = jnp.broadcast_to(code[0:1, :], (64, 128)).astype(I32)
        match = (code == (sub & 7)) & (((lane & 31) >> 2) == (sub >> 3))
        owner[:, 128 * h : 128 * (h + 1)] = jnp.where(match, 1.0, 0.0).astype(BF16)
    parts = split3(zrecv[...].reshape(256, 384))
    owners = owner[...]
    dense = dot_nn(owners, parts[0]) + dot_nn(owners, parts[1]) + dot_nn(owners, parts[2])
    xsend[...] = dense.reshape(NX, 8, 384)
    xcopies = []
    for i in range(1, NX):
        xx = lax.rem(x + i, NX)
        xcopies.append(remote(xsend.at[xx], xrecv.at[x], xss.at[i], xrs.at[x], row(xx)))
        xcopies[-1].start()
    xrecv[x] = xsend[x]

    for i in range(4):
        hcopies[i].wait_recv()
    zero_row = jnp.zeros((1, 128), F32)
    above, below = [], []
    for half in range(2):
        for b in range(4):
            above.append(jnp.where(seg > 0, row_recv[0, 4 * half + b : 4 * half + b + 1, :], zero_row))
            below.append(jnp.where(seg < n_seg - 1, row_recv[1, 4 * half + b : 4 * half + b + 1, :], zero_row))
    pres_above, perm_above = jnp.concatenate(above[:4], axis=1), jnp.concatenate(above[4:], axis=1)
    pres_below, perm_below = jnp.concatenate(below[:4], axis=1), jnp.concatenate(below[4:], axis=1)
    sides = jnp.concatenate(
        [
            jnp.where(me > 0, col_recv[0], 0.0),
            jnp.where(me < n_dev - 1, col_recv[1], 0.0),
            jnp.zeros((112, 128), F32),
        ],
        axis=0,
    ).T
    lane8 = iota((8, 512), 1)

    def edge_term(p, k, p2, k2):
        return (2.0 * k * k2 / (k + k2)) * (p - p2)

    for r in range(16):
        rows = slice(8 * r, 8 * (r + 1))
        p, k = pres[rows, :], perm[rows, :]
        if r == 0:
            pu = jnp.concatenate([pres_above, pres[0:7, :]], axis=0)
            ku = jnp.concatenate([perm_above, perm[0:7, :]], axis=0)
        else:
            pu, ku = pres[8 * r - 1 : 8 * r + 7, :], perm[8 * r - 1 : 8 * r + 7, :]
        if r == 15:
            pd = jnp.concatenate([pres[121:128, :], pres_below], axis=0)
            kd = jnp.concatenate([perm[121:128, :], perm_below], axis=0)
        else:
            pd, kd = pres[8 * r + 1 : 8 * r + 9, :], perm[8 * r + 1 : 8 * r + 9, :]
        side = sides[rows, :]
        pl_, kl_ = side[:, 7:8], side[:, 6:7]
        pr_, kr_ = side[:, 8:9], side[:, 9:10]
        pleft = jnp.where(lane8 == 0, pl_, pltpu.roll(p, 1, 1))
        kleft = jnp.where(lane8 == 0, kl_, pltpu.roll(k, 1, 1))
        pright = jnp.where(lane8 == 511, pr_, pltpu.roll(p, 511, 1))
        kright = jnp.where(lane8 == 511, kr_, pltpu.roll(k, 511, 1))
        total = COMPRESS * (p - prev[rows, :])
        total = total + edge_term(p, k, pd, kd) + edge_term(p, k, pu, ku)
        total = total + edge_term(p, k, pright, kright) + edge_term(p, k, pleft, kleft)
        flow[rows, :] = total
    flow_copy = pltpu.make_async_copy(flow, flow_o, osem.at[0])
    flow_copy.start()

    for i in range(1, NX):
        xx = lax.rem(x + i, NX)
        remote(xsend.at[xx], xrecv.at[xx], xss.at[i], xrs.at[xx], row(xx)).wait_recv()
    mortar_sum = xrecv[0]
    for i in range(1, NX):
        mortar_sum = mortar_sum + xrecv[i]
    jump = [uplus_r[:, c, :] - mortar_sum[:, 128 * c : 128 * (c + 1)] for c in range(3)]
    normal_part = PENALTY * jump[0]
    stress = CONFINING - node_p[...] - normal_part
    softplus = jnp.maximum(stress, 0.0) + jnp.log1p(jnp.exp(-jnp.abs(stress)))
    factor = FRICTION * softplus / jnp.sqrt(jump[1] * jump[1] + jump[2] * jump[2] + 1.0)
    state = state_r[...]
    sliding = [normal_part, jump[1] * factor, jump[2] * factor]
    traction = [
        jnp.where(state == 0, PENALTY * jump[c], jnp.where(state == 1, sliding[c], 0.0)) for c in range(3)
    ]
    for c in range(3):
        traction_o[:, 128 * c : 128 * (c + 1)] = traction[c]
    tsend[...] = jnp.concatenate(traction + [jnp.zeros((8, 128), F32)], axis=0).astype(BF16)
    tcopies = []
    for i in range(1, NX):
        xx = lax.rem(x + i, NX)
        tcopies.append(remote(tsend, trecv.at[x], tss.at[i], trs.at[x], row(xx)))
        tcopies[-1].start()
    trecv[x] = tsend[...]
    for i in range(1, NX):
        xx = lax.rem(x + i, NX)
        remote(tsend, trecv.at[xx], tss.at[i], trs.at[xx], row(xx)).wait_recv()

    got = trecv[...].astype(F32)
    table = jnp.concatenate([got[:, 8 * c : 8 * (c + 1), :].reshape(64, 128) for c in range(3)], axis=1)
    rsend[...] = dot_tn(owner[...], table.astype(BF16)).astype(BF16).reshape(NP, 32, 384)
    rcopies = []
    for i in range(1, NP):
        p = lax.rem(pos + i, NP)
        rcopies.append(remote(rsend.at[p], rrecv.at[pos], rss.at[i], rrs.at[pos], column(p)))
        rcopies[-1].start()
    rrecv[pos] = rsend[pos]
    for i in range(1, NP):
        p = lax.rem(pos + i, NP)
        remote(rsend.at[p], rrecv.at[p], rss.at[i], rrs.at[p], column(p)).wait_recv()
    pair_traction_o[...] = dot_nn(slots_t[...], rrecv[...].reshape(256, 384)).astype(BF16)

    for copy in ccopies + zcopies + hcopies + xcopies + tcopies + rcopies:
        copy.wait_send()
    flow_copy.wait()


def reaction_kernel(
    source_s, pair_traction_r, traction_r, flow_h, mortar_h, flow_o, traction_o, force_o, mort, msem, fsem
):
    copies = [
        pltpu.make_async_copy(mortar_h.at[pl.ds(8 * g, 8)], mort.at[pl.ds(8 * g, 8)], msem.at[g])
        for g in range(8)
    ]
    for copy in copies:
        copy.start()
    flow_copy = pltpu.make_async_copy(flow_h, flow_o, fsem)
    flow_copy.start()
    for c in range(3):
        traction_o[:, c, :] = traction_r[:, 128 * c : 128 * (c + 1)]
    patch = iota((8, 128), 0)
    total = jnp.zeros((32, 128), F32)
    for g in range(8):
        copies[g].wait()
        values = pair_traction_r[8 * g : 8 * (g + 1), :].astype(F32)
        for j in range(8):
            q = 8 * g + j
            mine = patch == source_s[q]
            rows = [
                jnp.where(mine, jnp.broadcast_to(values[j : j + 1, 128 * c : 128 * (c + 1)], (8, 128)), 0.0)
                for c in range(3)
            ]
            left = jnp.concatenate(rows + [jnp.zeros((8, 128), F32)], axis=0).astype(BF16)
            total = total + dot_nn(left, mort[q])
    for c in range(3):
        force_o[:, c, :] = -total[8 * c : 8 * (c + 1), :]
    flow_copy.wait()


def on_device(
    pressure, pressure_prev, permeability, u_plus, u_minus, node_state, node_cell,
    pair_source, pair_dest, pair_target, mortar,
):
    any_, vmem, smem = (pl.BlockSpec(memory_space=s) for s in (pl.ANY, pltpu.VMEM, pltpu.SMEM))
    dma = pltpu.SemaphoreType.DMA
    shape = jax.ShapeDtypeStruct
    pair_traction, traction, flow = pl.pallas_call(
        exchange_kernel,
        out_shape=(shape((64, 384), BF16), shape((8, 384), F32), shape((128, 512), F32)),
        in_specs=[any_, any_, any_, vmem, vmem, vmem, vmem, vmem, vmem, smem, any_],
        out_specs=(vmem, vmem, any_),
        scratch_shapes=[
            pltpu.VMEM((128, 512), F32),
            pltpu.VMEM((128, 512), F32),
            pltpu.VMEM((128, 512), F32),
            pltpu.VMEM((64, 128, 128), BF16),
            pltpu.VMEM((128, 512), F32),
            pltpu.VMEM((64, 384), F32),
            pltpu.VMEM((64, 256), BF16),
            pltpu.VMEM((64, 256), BF16),
            pltpu.VMEM((NP, 32, 384), F32),
            pltpu.VMEM((NP, 32, 384), F32),
            pltpu.VMEM((NP, 8, 128), F32),
            pltpu.VMEM((NP, 8, 128), F32),
            pltpu.VMEM((NX, 8, 384), F32),
            pltpu.VMEM((NX, 8, 384), F32),
            pltpu.VMEM((32, 128), BF16),
            pltpu.VMEM((NX, 32, 128), BF16),
            pltpu.VMEM((NP, 32, 384), BF16),
            pltpu.VMEM((NP, 32, 384), BF16),
            pltpu.VMEM((2, 8, 128), F32),
            pltpu.VMEM((2, 8, 128), F32),
            pltpu.VMEM((2, 8, 128), F32),
            pltpu.VMEM((2, 8, 128), F32),
            pltpu.VMEM((8, 128), F32),
            dma((8,)), dma((3,)),
            dma((8,)), dma((8,)), dma((8,)), dma((8,)), dma((8,)), dma((8,)),
            dma((8,)), dma((8,)), dma((8,)), dma((8,)), dma((4,)), dma((4,)), dma((1,)),
        ],
        compiler_params=pltpu.CompilerParams(
            collective_id=0, has_side_effects=True, vmem_limit_bytes=32 * 1024 * 1024
        ),
        name="exchange",
    )(
        pressure, pressure_prev, permeability, u_plus, u_minus, node_state, node_cell,
        pair_dest.reshape(64), pair_target, pair_source, mortar,
    )
    return pl.pallas_call(
        reaction_kernel,
        out_shape=(shape((128, 512), F32), shape((8, 3, 128), F32), shape((8, 3, 128), F32)),
        in_specs=[smem, vmem, vmem, any_, any_],
        out_specs=(any_, vmem, vmem),
        scratch_shapes=[pltpu.VMEM((64, 128, 128), BF16), dma((8,)), dma],
        compiler_params=pltpu.CompilerParams(vmem_limit_bytes=32 * 1024 * 1024),
        name="reaction",
    )(pair_source, pair_traction, traction, flow, mortar)


def solution(mesh):
    both = ("seg", "dev")
    cells, patches = P("seg", "dev"), P(both, None, None)
    placed = (
        cells, cells, cells, patches, patches, P(both, None), P(both, None), P(both), P(both, None), P(both), patches,
    )
    return jax.shard_map(
        on_device, mesh=mesh, in_specs=placed, out_specs=(cells, patches, patches), check_vma=False
    )
```

time: 83.8 us -> 54.9 us (0.66)
  starting transfers between devices: 47.3 us -> 0 us
  Pallas kernels: 0 us -> 43.5 us
  waiting for transfers between devices: 10.9 us -> 0 us
  other arithmetic: 8.51 us -> 0 us
  matrix products: 3.55 us -> 0 us
  local copies, waits for them, and re-layouts: 11.5 us -> 10.4 us
    pallas_call x0 -> x2, Pallas kernels: none -> 43.5 us  [the longest x1 41.3 us: on_device(): pl.pallas_call(exchange_kernel, out_shape=(shape((64, 384), BF16), shape(...]
    all_to_all x3 -> x0, starting transfers between devices: 36.5 us -> none  [the longest x1 14.8 us: on_device(): lax.all_to_all(target_slots.reshape(peer_count, CAP), 'dev', split_axis=0...]
    all_to_all x3 -> x0, waiting for transfers between devices: 10.9 us -> none  [the longest x1 9.81 us: on_device(): lax.all_to_all(reply_slots.reshape(peer_count, CAP, 3, node_count), 'dev'...]
    ppermute x4 -> x0, starting transfers between devices: 10.8 us -> none  [the longest x2 7.19 us: extended(): before = lax.ppermute(last, axis, up)]
    unnamed x21 -> x22, local copies, waits for them, and re-layouts: 0.14 us -> 9.19 us
    gather x3 -> x0, local copies, waits for them, and re-layouts: 8.29 us -> none  [the longest x1 6.15 us: on_device(): node_pressure = pressure.reshape(-1)[node_cell]]
    dot_general x6 -> x0, matrix products: 3.55 us -> none  [the longest x1 1.17 us: on_device(): jnp.einsum('pij,pcj->pci', mortar, minus_rows, preferred_element_type=jnp...]
    add x3 -> x0, other arithmetic: 2.83 us -> none  [the longest x1 2.16 us: cell_residual(): total = total + conduct * (pressure - neighbor_p)]
  transfers between devices with their start and end apart: 7 -> 0, of which waited for: 2 -> 0; matrix products, arithmetic and copies ran while one was open for 21% -> 0% of each run, Pallas kernels for 0% -> 0%
where the time goes in v1:
time: 54.9 us; the launch traced here: 54.5 us
  Pallas kernels  43.5 us (79%)
  local copies, waits for them, and re-layouts  10.4 us (19%)
  between operations  0.67 us (1%)
    pallas_call x1, Pallas kernels, on_device(): pl.pallas_call(exchange_kernel, out_shape=(shape((64, 384), BF16), shape(...  41.3 us
    unnamed x22, local copies, waits for them, and re-layouts  9.19 us
    pallas_call x1, Pallas kernels, on_device(): pl.pallas_call(reaction_kernel, out_shape=(shape((128, 512), F32), shape(...  2.12 us
    pallas_call x2, local copies, waits for them, and re-layouts, on_device(): pl.pallas_call(reaction_kernel, out_shape=(shape((128, 512), F32), shape(...  1.2 us

profile of v1, /device:TPU:1, one launch (start us, length us, event | category | flops | bytes accessed | tf_op | source)
XLA Modules:
  0.0 54.5 jit_solution(16044138090266084835)
XLA Ops:
  0.6 0.7 %copy.15.uminus_r = bf16[8,3,128]{2,1,0:T(4,128)(2,1)S(1)} copy(bf16[8,3,128]{2,0,1:T(8,128)(2,1)} %param.15) | data formatting | bytes 12288 | tf_op args[4]
  1.3 0.7 %copy.14.uplus_r = f32[8,3,128]{2,1,0:T(4,128)S(1)} copy(f32[8,3,128]{2,0,1:T(8,128)} %param.14) | data formatting | bytes 24576 | tf_op args[3]
  2.0 0.0 copy-start
  2.0 1.6 %copy-done = bf16[64,128,128]{2,1,0:T(8,128)(2,1)S(1)} copy-done((bf16[64,128,128]{2,1,0:T(8,128)(2,1)S(1)}, bf16[64,128,128]{2,1,0:T(8,128)(2,1)}, u32[]{:S(2)}) %copy-start) | copy-done | bytes 2097176
  3.6 0.0 copy-start.2
  3.6 0.9 %copy-done.2 = f32[128,512]{1,0:T(8,128)S(1)} copy-done((f32[128,512]{1,0:T(8,128)S(1)}, f32[128,512]{1,0:T(8,128)}, u32[]{:S(2)}) %copy-start.2) | copy-done | bytes 262168
  4.6 0.0 copy-start.3
  4.6 0.9 %copy-done.3 = f32[128,512]{1,0:T(8,128)S(1)} copy-done((f32[128,512]{1,0:T(8,128)S(1)}, f32[128,512]{1,0:T(8,128)}, u32[]{:S(2)}) %copy-start.3) | copy-done | bytes 262168
  5.5 0.0 copy-start.4
  5.5 0.9 %copy-done.4 = f32[128,512]{1,0:T(8,128)S(1)} copy-done((f32[128,512]{1,0:T(8,128)S(1)}, f32[128,512]{1,0:T(8,128)}, u32[]{:S(2)}) %copy-start.4) | copy-done | bytes 262168
  6.5 0.0 copy-start.5
  6.5 0.7 %copy-done.5 = s32[8,128]{1,0:T(8,128)S(1)} copy-done((s32[8,128]{1,0:T(8,128)S(1)}, s32[8,128]{1,0:T(8,128)}, u32[]{:S(2)}) %copy-start.5) | copy-done | bytes 4120
  7.2 0.7 %copy-done.6 = s32[8,128]{1,0:T(8,128)S(1)} copy-done((s32[8,128]{1,0:T(8,128)S(1)}, s32[8,128]{1,0:T(8,128)}, u32[]{:S(2)}) %copy-start.6) | copy-done | bytes 4120
  7.9 0.0 copy-start.7
  7.9 0.7 %copy-done.7 = s32[64]{0:T(128)S(1)} copy-done((s32[64]{0:T(128)S(1)}, s32[64]{0:T(128)}, u32[]{:S(2)}) %copy-start.7) | copy-done | bytes 280
  8.5 0.0 copy-start.8
  8.5 0.7 %copy-done.8 = s32[64,1]{0,1:T(1,128)S(1)} copy-done((s32[64,1]{0,1:T(1,128)S(1)}, s32[64,1]{0,1:T(1,128)}, u32[]{:S(2)}) %copy-start.8) | copy-done | bytes 280
  9.2 0.0 copy-start.9
  9.2 0.7 %copy-done.9 = s32[64]{0:T(128)S(1)} copy-done((s32[64]{0:T(128)S(1)}, s32[64]{0:T(128)}, u32[]{:S(2)}) %copy-start.9) | copy-done | bytes 280
  9.8 41.3 %exchange.1 = (bf16[64,384]{1,0:T(8,128)(2,1)S(1)}, f32[8,384]{1,0:T(8,128)S(1)}, f32[128,512]{1,0:T(8,128)S(1)}) custom-call(f32[128,512]{1,0:T(8,128)S(1)} %copy-done.2, f32[128,512]{1,0:T(8,128)S(1)} %copy-done.3, f32[128,512]{1,0:T(8,128)S(1)} %copy-done.4, f32[8,3,128]{2,1,0:T(4,128)S(1)} %copy.14.uplus_r, bf16[8,3,128]{2,1,0:T(4,128)(2,1)S(1)} %copy.15.uminus_r, ...), custom_call_target="tpu_custom_call" | custom-call | tf_op jit(solution)/shard_map/exchange/pallas_call | solution.py:345
  51.2 0.0 copy-done.1
  51.2 2.1 %reaction.1 = (f32[128,512]{1,0:T(8,128)}, f32[8,3,128]{2,1,0:T(4,128)S(1)}, f32[8,3,128]{2,1,0:T(4,128)S(1)}) custom-call(s32[64]{0:T(128)S(1)} %copy-done.7, bf16[64,384]{1,0:T(8,128)(2,1)S(1)} %get-tuple-element.6.pair_traction_r, f32[8,384]{1,0:T(8,128)S(1)} %get-tuple-element.7.traction_r, f32[128,512]{1,0:T(8,128)S(1)} %get-tuple-element.8.flow_h, ...), custom_call_target="tpu_custom_call" | custom-call | tf_op jit(solution)/shard_map/reaction/pallas_call | solution.py:386
  53.3 0.6 %copy.16 = f32[8,3,128]{2,0,1:T(8,128)} copy(f32[8,3,128]{2,1,0:T(4,128)S(1)} %get-tuple-element.10) | data formatting | bytes 24576 | tf_op jit(solution)/shard_map/reaction/pallas_call | solution.py:386
  53.9 0.6 %copy.17 = f32[8,3,128]{2,0,1:T(8,128)} copy(f32[8,3,128]{2,1,0:T(4,128)S(1)} %get-tuple-element.11) | data formatting | bytes 24576 | tf_op jit(solution)/shard_map/reaction/pallas_call | solution.py:386
  (2 shorter events, 0.0 us)
Async XLA Ops:
  2.0 1.6 %copy-start = (bf16[64,128,128]{2,1,0:T(8,128)(2,1)S(1)}, bf16[64,128,128]{2,1,0:T(8,128)(2,1)}, u32[]{:S(2)}) copy-start(bf16[64,128,128]{2,1,0:T(8,128)(2,1)} %mortar_h.3) | copy-start | bytes 6291460
  3.6 0.9 %copy-start.2 = (f32[128,512]{1,0:T(8,128)S(1)}, f32[128,512]{1,0:T(8,128)}, u32[]{:S(2)}) copy-start(f32[128,512]{1,0:T(8,128)} %pressure_h.1) | copy-start | bytes 786436
  4.6 0.9 %copy-start.3 = (f32[128,512]{1,0:T(8,128)S(1)}, f32[128,512]{1,0:T(8,128)}, u32[]{:S(2)}) copy-start(f32[128,512]{1,0:T(8,128)} %prev_h.1) | copy-start | bytes 786436
  5.5 0.9 %copy-start.4 = (f32[128,512]{1,0:T(8,128)S(1)}, f32[128,512]{1,0:T(8,128)}, u32[]{:S(2)}) copy-start(f32[128,512]{1,0:T(8,128)} %perm_h.1) | copy-start | bytes 786436
  6.5 0.7 %copy-start.5 = (s32[8,128]{1,0:T(8,128)S(1)}, s32[8,128]{1,0:T(8,128)}, u32[]{:S(2)}) copy-start(s32[8,128]{1,0:T(8,128)} %state_r.1) | copy-start | bytes 12292
  7.2 0.7 %copy-start.6 = (s32[8,128]{1,0:T(8,128)S(1)}, s32[8,128]{1,0:T(8,128)}, u32[]{:S(2)}) copy-start(s32[8,128]{1,0:T(8,128)} %cell_r.1) | copy-start | bytes 12292
  7.9 0.7 %copy-start.7 = (s32[64]{0:T(128)S(1)}, s32[64]{0:T(128)}, u32[]{:S(2)}) copy-start(s32[64]{0:T(128)} %source_s.3) | copy-start | bytes 772
  8.5 0.7 %copy-start.8 = (s32[64,1]{0,1:T(1,128)S(1)}, s32[64,1]{0,1:T(1,128)}, u32[]{:S(2)}) copy-start(s32[64,1]{0,1:T(1,128)} %param.19) | copy-start | bytes 772
  9.2 0.7 %copy-start.9 = (s32[64]{0:T(128)S(1)}, s32[64]{0:T(128)}, u32[]{:S(2)}) copy-start(s32[64]{0:T(128)} %target_r.1) | copy-start | bytes 772
  9.8 41.4 %copy-start.1 = (bf16[64,128,128]{2,1,0:T(8,128)(2,1)S(1)}, bf16[64,128,128]{2,1,0:T(8,128)(2,1)}, u32[]{:S(2)}) copy-start(bf16[64,128,128]{2,1,0:T(8,128)(2,1)} %mortar_h.3) | copy-start | bytes 6291460

commit v2 on v1

--- a/solution.py
+++ b/solution.py
@@ -11,11 +11,12 @@
 FRICTION = 0.6
 CONFINING = 1.0
 
-NX = 8
 NP = 8
+NZ = 8
 F32 = jnp.float32
 BF16 = jnp.bfloat16
 I32 = jnp.int32
+I16 = jnp.int16
 MESH = pl.DeviceIdType.MESH
 
 
@@ -23,12 +24,9 @@
     return lax.broadcasted_iota(I32, shape, dim)
 
 
-def split3(value):
+def split2(value):
     high = value.astype(BF16)
-    rest = value - high.astype(F32)
-    mid = rest.astype(BF16)
-    low = (rest - mid.astype(F32)).astype(BF16)
-    return high, mid, low
+    return high, (value - high.astype(F32)).astype(BF16)
 
 
 def dot_nn(a, b):
@@ -50,48 +48,57 @@
 
 
 def exchange_kernel(
-    pressure_h, prev_h, perm_h, uplus_r, uminus_r, state_r, cell_r, dest_r, target_r, source_s, mortar_h,
-    pair_traction_o, traction_o, flow_o,
-    pres, prev, perm, mort, flow, proj, slots_t, owner, zsend, zrecv, csend, crecv, xsend, xrecv,
+    pressure_h, prev_h, perm_h, uplus_h, uminus_h, state_h, cell_h, dest_h, target_h, source_h, mortar_h,
+    faces_o, flow_o,
+    pres, prev, perm, mort, flow, proj, slots_t, owner, weight, zsend, zrecv, csend, crecv, xsend, xrecv,
     tsend, trecv, rsend, rrecv, row_send, row_recv, col_send, col_recv, node_p,
-    msem, lsem, zss, zrs, css, crs, xss, xrs, tss, trs, rss, rrs, hss, hrs, osem,
+    uplus_r, uminus_r, state_r, cell_r, dest_r, target_r, source_s, by_patch,
+    fsem, msem, lsem, zss, zrs, css, crs, xss, xrs, tss, trs, rss, rrs, hss, hrs, osem,
 ):
     seg = lax.axis_index("seg")
     me = lax.axis_index("dev")
     n_seg = lax.axis_size("seg")
     n_dev = lax.axis_size("dev")
-    x = lax.rem(me // 2, NX)
-    pos = (me // (2 * NX)) * 2 + lax.rem(me, 2)
+    z, pos = me // NP, lax.rem(me, NP)
 
     def column(p):
-        return {"dev": (p // 2) * (2 * NX) + x * 2 + lax.rem(p, 2)}
-
-    def row(xx):
-        return {"dev": (pos // 2) * (2 * NX) + xx * 2 + lax.rem(pos, 2)}
+        return {"dev": z * NP + p}
+
+    def row(zz):
+        return {"dev": zz * NP + pos}
 
     seg_up, seg_down = {"seg": lax.rem(seg + 1, n_seg)}, {"seg": lax.rem(seg + n_seg - 1, n_seg)}
     dev_up, dev_down = {"dev": lax.rem(me + 1, n_dev)}, {"dev": lax.rem(me + n_dev - 1, n_dev)}
 
-    mcopies = [
-        pltpu.make_async_copy(mortar_h.at[pl.ds(8 * g, 8)], mort.at[pl.ds(8 * g, 8)], msem.at[g])
-        for g in range(8)
-    ]
-    for copy in mcopies:
-        copy.start()
-    lcopies = [
-        pltpu.make_async_copy(a, b, lsem.at[i])
-        for i, (a, b) in enumerate(((pressure_h, pres), (perm_h, perm), (prev_h, prev)))
-    ]
-    for copy in lcopies:
-        copy.start()
+    def fetch(pairs, sems):
+        copies = [pltpu.make_async_copy(a, b, sems.at[i]) for i, (a, b) in enumerate(pairs)]
+        for copy in copies:
+            copy.start()
+        return copies
+
+    first = fetch(((dest_h, dest_r), (target_h, target_r), (source_h, source_s), (uminus_h, uminus_r)), fsem)
+    mcopies = fetch([(mortar_h.at[pl.ds(8 * g, 8)], mort.at[pl.ds(8 * g, 8)]) for g in range(8)], msem)
+    lcopies = fetch(
+        (
+            (pressure_h, pres), (cell_h, cell_r), (perm_h, perm), (prev_h, prev),
+            (uplus_h, uplus_r), (state_h, state_r),
+        ),
+        lsem,
+    )
 
     barrier = pltpu.get_barrier_semaphore()
     for i in range(1, NP):
         pl.semaphore_signal(barrier, inc=1, device_id=column(lax.rem(pos + i, NP)), device_id_type=MESH)
-    for i in range(1, NX):
-        pl.semaphore_signal(barrier, inc=1, device_id=row(lax.rem(x + i, NX)), device_id_type=MESH)
+    for i in range(1, NZ):
+        pl.semaphore_signal(barrier, inc=1, device_id=row(lax.rem(z + i, NZ)), device_id_type=MESH)
     for device in (seg_up, seg_down, dev_up, dev_down):
         pl.semaphore_signal(barrier, inc=1, device_id=device, device_id_type=MESH)
+
+    for copy in first:
+        copy.wait()
+    for b in range(8):
+        for c in range(3):
+            by_patch[b, c : c + 1, :] = uminus_r[c].astype(F32)[b : b + 1, :]
 
     lane, sub = iota((64, 128), 1), iota((64, 128), 0)
     diagonal = lane == sub
@@ -104,30 +111,32 @@
     dest_row, dest = as_column(dest_r)
     _, target = as_column(target_r)
     rank = jnp.sum(jnp.where((dest_row == dest) & (lane < sub), 1, 0), axis=1, keepdims=True)
-    slot = (((dest >> 4) * 2 + (dest & 1)) * NX + ((dest >> 1) & (NX - 1))) * CAP + rank
+    slot = ((dest & (NP - 1)) * NZ + (dest >> 3)) * CAP + rank
     for h in range(2):
         slots_t[:, 128 * h : 128 * (h + 1)] = jnp.where(slot == lane + 128 * h, 1.0, 0.0).astype(BF16)
-    for p in range(NP):
-        code = jnp.sum(jnp.where(slot == (lane & 31) + 32 * p, target, 0), axis=0, keepdims=True)
-        csend[p] = jnp.broadcast_to(code.astype(F32), (8, 128))
-
     for g in range(8):
         mcopies[g].wait()
 
         def project(j, carry):
             q = 8 * g + j
-            value = dot_nt(uminus_r[source_s[q]], mort[q])
+            value = dot_nt(by_patch[source_s[q]].astype(BF16), mort[q])
             for c in range(3):
                 proj[pl.ds(q, 1), 128 * c : 128 * (c + 1)] = value[c : c + 1, :]
             return carry
 
         lax.fori_loop(0, 8, project, 0, unroll=True)
-    parts = split3(proj[...])
+    size = jnp.max(jnp.abs(proj[...]), axis=1, keepdims=True)
+    power = jnp.floor(jnp.log2(jnp.maximum(size, 1e-30))) + 1.0
+    whole = jnp.clip(jnp.round(proj[...] * jnp.exp2(15.0 - power)), -32767.0, 32767.0)
+    label = target.astype(F32) + 8.0 * (power + 128.0)
+    for p in range(NP):
+        code = jnp.sum(jnp.where(slot == (lane & 31) + 32 * p, label, 0.0), axis=0, keepdims=True)
+        csend[p] = jnp.broadcast_to(code, (8, 128))
+    high, low = split2(whole)
     hit = slots_t[...]
-    placed = dot_tn(hit, parts[0]) + dot_tn(hit, parts[1]) + dot_tn(hit, parts[2])
-    zsend[...] = placed.reshape(NP, 32, 384)
-
-    pl.semaphore_wait(barrier, NP - 1 + NX - 1 + 4)
+    zsend[...] = (dot_tn(hit, high) + dot_tn(hit, low)).astype(I32).astype(I16).reshape(NP, 32, 384)
+
+    pl.semaphore_wait(barrier, NP - 1 + NZ - 1 + 4)
 
     zcopies, ccopies = [], []
     for i in range(1, NP):
@@ -192,18 +201,20 @@
         for p in range(4):
             code = jnp.where((iota((8, 128), 1) >> 5) == p, crecv[4 * h + p], code)
         code = jnp.broadcast_to(code[0:1, :], (64, 128)).astype(I32)
-        match = (code == (sub & 7)) & (((lane & 31) >> 2) == (sub >> 3))
+        scale = jnp.exp2((code >> 3).astype(F32) - (128.0 + 15.0))
+        match = ((code & 7) == (sub & 7)) & (((lane & 31) >> 2) == (sub >> 3))
         owner[:, 128 * h : 128 * (h + 1)] = jnp.where(match, 1.0, 0.0).astype(BF16)
-    parts = split3(zrecv[...].reshape(256, 384))
-    owners = owner[...]
-    dense = dot_nn(owners, parts[0]) + dot_nn(owners, parts[1]) + dot_nn(owners, parts[2])
-    xsend[...] = dense.reshape(NX, 8, 384)
+        weight[:, 128 * h : 128 * (h + 1)] = jnp.where(match, scale, 0.0).astype(BF16)
+    high, low = split2(zrecv[...].reshape(256, 384).astype(I32).astype(F32))
+    weights = weight[...]
+    dense = dot_nn(weights, high) + dot_nn(weights, low)
+    xsend[...] = dense.reshape(NZ, 8, 384)
     xcopies = []
-    for i in range(1, NX):
-        xx = lax.rem(x + i, NX)
-        xcopies.append(remote(xsend.at[xx], xrecv.at[x], xss.at[i], xrs.at[x], row(xx)))
+    for i in range(1, NZ):
+        zz = lax.rem(z + i, NZ)
+        xcopies.append(remote(xsend.at[zz], xrecv.at[z], xss.at[i], xrs.at[z], row(zz)))
         xcopies[-1].start()
-    xrecv[x] = xsend[x]
+    xrecv[z] = xsend[z]
 
     for i in range(4):
         hcopies[i].wait_recv()
@@ -255,13 +266,13 @@
     flow_copy = pltpu.make_async_copy(flow, flow_o, osem.at[0])
     flow_copy.start()
 
-    for i in range(1, NX):
-        xx = lax.rem(x + i, NX)
-        remote(xsend.at[xx], xrecv.at[xx], xss.at[i], xrs.at[xx], row(xx)).wait_recv()
+    for i in range(1, NZ):
+        zz = lax.rem(z + i, NZ)
+        remote(xsend.at[zz], xrecv.at[zz], xss.at[i], xrs.at[zz], row(zz)).wait_recv()
     mortar_sum = xrecv[0]
-    for i in range(1, NX):
+    for i in range(1, NZ):
         mortar_sum = mortar_sum + xrecv[i]
-    jump = [uplus_r[:, c, :] - mortar_sum[:, 128 * c : 128 * (c + 1)] for c in range(3)]
+    jump = [uplus_r[c] - mortar_sum[:, 128 * c : 128 * (c + 1)] for c in range(3)]
     normal_part = PENALTY * jump[0]
     stress = CONFINING - node_p[...] - normal_part
     softplus = jnp.maximum(stress, 0.0) + jnp.log1p(jnp.exp(-jnp.abs(stress)))
@@ -272,17 +283,17 @@
         jnp.where(state == 0, PENALTY * jump[c], jnp.where(state == 1, sliding[c], 0.0)) for c in range(3)
     ]
     for c in range(3):
-        traction_o[:, 128 * c : 128 * (c + 1)] = traction[c]
+        faces_o[c] = traction[c]
     tsend[...] = jnp.concatenate(traction + [jnp.zeros((8, 128), F32)], axis=0).astype(BF16)
     tcopies = []
-    for i in range(1, NX):
-        xx = lax.rem(x + i, NX)
-        tcopies.append(remote(tsend, trecv.at[x], tss.at[i], trs.at[x], row(xx)))
+    for i in range(1, NZ):
+        zz = lax.rem(z + i, NZ)
+        tcopies.append(remote(tsend, trecv.at[z], tss.at[i], trs.at[z], row(zz)))
         tcopies[-1].start()
-    trecv[x] = tsend[...]
-    for i in range(1, NX):
-        xx = lax.rem(x + i, NX)
-        remote(tsend, trecv.at[xx], tss.at[i], trs.at[xx], row(xx)).wait_recv()
+    trecv[z] = tsend[...]
+    for i in range(1, NZ):
+        zz = lax.rem(z + i, NZ)
+        remote(tsend, trecv.at[zz], tss.at[i], trs.at[zz], row(zz)).wait_recv()
 
     got = trecv[...].astype(F32)
     table = jnp.concatenate([got[:, 8 * c : 8 * (c + 1), :].reshape(64, 128) for c in range(3)], axis=1)
@@ -296,31 +307,12 @@
     for i in range(1, NP):
         p = lax.rem(pos + i, NP)
         remote(rsend.at[p], rrecv.at[p], rss.at[i], rrs.at[p], column(p)).wait_recv()
-    pair_traction_o[...] = dot_nn(slots_t[...], rrecv[...].reshape(256, 384)).astype(BF16)
-
-    for copy in ccopies + zcopies + hcopies + xcopies + tcopies + rcopies:
-        copy.wait_send()
-    flow_copy.wait()
-
-
-def reaction_kernel(
-    source_s, pair_traction_r, traction_r, flow_h, mortar_h, flow_o, traction_o, force_o, mort, msem, fsem
-):
-    copies = [
-        pltpu.make_async_copy(mortar_h.at[pl.ds(8 * g, 8)], mort.at[pl.ds(8 * g, 8)], msem.at[g])
-        for g in range(8)
-    ]
-    for copy in copies:
-        copy.start()
-    flow_copy = pltpu.make_async_copy(flow_h, flow_o, fsem)
-    flow_copy.start()
-    for c in range(3):
-        traction_o[:, c, :] = traction_r[:, 128 * c : 128 * (c + 1)]
+    proj[...] = dot_nn(slots_t[...], rrecv[...].reshape(256, 384))
+
     patch = iota((8, 128), 0)
     total = jnp.zeros((32, 128), F32)
     for g in range(8):
-        copies[g].wait()
-        values = pair_traction_r[8 * g : 8 * (g + 1), :].astype(F32)
+        values = proj[8 * g : 8 * (g + 1), :]
         for j in range(8):
             q = 8 * g + j
             mine = patch == source_s[q]
@@ -331,22 +323,43 @@
             left = jnp.concatenate(rows + [jnp.zeros((8, 128), F32)], axis=0).astype(BF16)
             total = total + dot_nn(left, mort[q])
     for c in range(3):
-        force_o[:, c, :] = -total[8 * c : 8 * (c + 1), :]
+        faces_o[3 + c] = -total[8 * c : 8 * (c + 1), :]
+
+    for copy in ccopies + zcopies + hcopies + xcopies + tcopies + rcopies:
+        copy.wait_send()
     flow_copy.wait()
+
+
+def store_kernel(faces_h, flow_h, flow_o, traction_o, force_o, faces, flow, lsem, osem):
+    loads = [pltpu.make_async_copy(faces_h, faces, lsem.at[0]), pltpu.make_async_copy(flow_h, flow, lsem.at[1])]
+    stores = [
+        pltpu.make_async_copy(faces.at[pl.ds(0, 3)], traction_o, osem.at[0]),
+        pltpu.make_async_copy(faces.at[pl.ds(3, 3)], force_o, osem.at[1]),
+        pltpu.make_async_copy(flow, flow_o, osem.at[2]),
+    ]
+    for copy in loads:
+        copy.start()
+    loads[0].wait()
+    stores[0].start()
+    stores[1].start()
+    loads[1].wait()
+    stores[2].start()
+    for copy in stores:
+        copy.wait()
 
 
 def on_device(
     pressure, pressure_prev, permeability, u_plus, u_minus, node_state, node_cell,
     pair_source, pair_dest, pair_target, mortar,
 ):
-    any_, vmem, smem = (pl.BlockSpec(memory_space=s) for s in (pl.ANY, pltpu.VMEM, pltpu.SMEM))
+    hbm, vmem = (pl.BlockSpec(memory_space=s) for s in (pltpu.HBM, pltpu.VMEM))
     dma = pltpu.SemaphoreType.DMA
     shape = jax.ShapeDtypeStruct
-    pair_traction, traction, flow = pl.pallas_call(
+    faces, flow = pl.pallas_call(
         exchange_kernel,
-        out_shape=(shape((64, 384), BF16), shape((8, 384), F32), shape((128, 512), F32)),
-        in_specs=[any_, any_, any_, vmem, vmem, vmem, vmem, vmem, vmem, smem, any_],
-        out_specs=(vmem, vmem, any_),
+        out_shape=(shape((6, 8, 128), F32), shape((128, 512), F32)),
+        in_specs=[hbm] * 11,
+        out_specs=(vmem, hbm),
         scratch_shapes=[
             pltpu.VMEM((128, 512), F32),
             pltpu.VMEM((128, 512), F32),
@@ -356,14 +369,15 @@
             pltpu.VMEM((64, 384), F32),
             pltpu.VMEM((64, 256), BF16),
             pltpu.VMEM((64, 256), BF16),
-            pltpu.VMEM((NP, 32, 384), F32),
-            pltpu.VMEM((NP, 32, 384), F32),
+            pltpu.VMEM((64, 256), BF16),
+            pltpu.VMEM((NP, 32, 384), I16),
+            pltpu.VMEM((NP, 32, 384), I16),
             pltpu.VMEM((NP, 8, 128), F32),
             pltpu.VMEM((NP, 8, 128), F32),
-            pltpu.VMEM((NX, 8, 384), F32),
-            pltpu.VMEM((NX, 8, 384), F32),
+            pltpu.VMEM((NZ, 8, 384), F32),
+            pltpu.VMEM((NZ, 8, 384), F32),
             pltpu.VMEM((32, 128), BF16),
-            pltpu.VMEM((NX, 32, 128), BF16),
+            pltpu.VMEM((NZ, 32, 128), BF16),
             pltpu.VMEM((NP, 32, 384), BF16),
             pltpu.VMEM((NP, 32, 384), BF16),
             pltpu.VMEM((2, 8, 128), F32),
@@ -371,27 +385,36 @@
             pltpu.VMEM((2, 8, 128), F32),
             pltpu.VMEM((2, 8, 128), F32),
             pltpu.VMEM((8, 128), F32),
-            dma((8,)), dma((3,)),
+            pltpu.VMEM((3, 8, 128), F32),
+            pltpu.VMEM((3, 8, 128), BF16),
+            pltpu.VMEM((8, 128), I32),
+            pltpu.VMEM((8, 128), I32),
+            pltpu.VMEM((64,), I32),
+            pltpu.VMEM((64,), I32),
+            pltpu.SMEM((64,), I32),
+            pltpu.VMEM((8, 8, 128), F32),
+            dma((4,)), dma((8,)), dma((6,)),
             dma((8,)), dma((8,)), dma((8,)), dma((8,)), dma((8,)), dma((8,)),
             dma((8,)), dma((8,)), dma((8,)), dma((8,)), dma((4,)), dma((4,)), dma((1,)),
         ],
         compiler_params=pltpu.CompilerParams(
-            collective_id=0, has_side_effects=True, vmem_limit_bytes=32 * 1024 * 1024
+            collective_id=0, has_side_effects=True, vmem_limit_bytes=60 * 1024 * 1024
         ),
         name="exchange",
     )(
-        pressure, pressure_prev, permeability, u_plus, u_minus, node_state, node_cell,
-        pair_dest.reshape(64), pair_target, pair_source, mortar,
-    )
-    return pl.pallas_call(
-        reaction_kernel,
-        out_shape=(shape((128, 512), F32), shape((8, 3, 128), F32), shape((8, 3, 128), F32)),
-        in_specs=[smem, vmem, vmem, any_, any_],
-        out_specs=(any_, vmem, vmem),
-        scratch_shapes=[pltpu.VMEM((64, 128, 128), BF16), dma((8,)), dma],
-        compiler_params=pltpu.CompilerParams(vmem_limit_bytes=32 * 1024 * 1024),
-        name="reaction",
-    )(pair_source, pair_traction, traction, flow, mortar)
+        pressure, pressure_prev, permeability, u_plus.transpose(1, 0, 2), u_minus.transpose(1, 0, 2),
+        node_state, node_cell, pair_dest.reshape(64), pair_target, pair_source, mortar,
+    )
+    flow, traction, force = pl.pallas_call(
+        store_kernel,
+        out_shape=(shape((128, 512), F32), shape((3, 8, 128), F32), shape((3, 8, 128), F32)),
+        in_specs=[hbm, hbm],
+        out_specs=(hbm, hbm, hbm),
+        scratch_shapes=[pltpu.VMEM((6, 8, 128), F32), pltpu.VMEM((128, 512), F32), dma((2,)), dma((3,))],
+        compiler_params=pltpu.CompilerParams(vmem_limit_bytes=60 * 1024 * 1024),
+        name="store",
+    )(faces, flow)
+    return flow, traction.transpose(1, 0, 2), force.transpose(1, 0, 2)
 
 
 def solution(mesh):

time: 54.9 us -> 38.2 us (0.70)
  local copies, waits for them, and re-layouts: 10.4 us -> 0 us
  Pallas kernels: 43.5 us -> 37.4 us
    unnamed x22 -> x0, local copies, waits for them, and re-layouts: 9.19 us -> none
    pallas_call x2, Pallas kernels: 43.5 us -> 37.4 us  [the longest x1 35.7 us: on_device(): pl.pallas_call(exchange_kernel, out_shape=(shape((6, 8, 128), F32), shape...]
    pallas_call x2 -> x0, local copies, waits for them, and re-layouts: 1.2 us -> none  [on_device(): pl.pallas_call(reaction_kernel, out_shape=(shape((128, 512), F32), shape(...]
where the time goes in v2:
time: 38.2 us; the launch traced here: 38 us
  Pallas kernels  37.4 us (98%)
  between operations  0.64 us (2%)
    pallas_call x1, Pallas kernels, on_device(): pl.pallas_call(exchange_kernel, out_shape=(shape((6, 8, 128), F32), shape...  35.7 us
    pallas_call x1, Pallas kernels, on_device(): pl.pallas_call(store_kernel, out_shape=(shape((128, 512), F32), shape((3,...  1.71 us

profile of v2, /device:TPU:1, one launch (start us, length us, event | category | flops | bytes accessed | tf_op | source)
XLA Modules:
  0.0 38.0 jit_solution(1236999919799098795)
XLA Ops:
  0.6 35.7 %exchange.1 = (f32[6,8,128]{2,1,0:T(8,128)}, f32[128,512]{1,0:T(8,128)}) custom-call(f32[128,512]{1,0:T(8,128)} %pressure_h.1, f32[128,512]{1,0:T(8,128)} %prev_h.1, f32[128,512]{1,0:T(8,128)} %perm_h.1, f32[3,8,128]{2,1,0:T(8,128)} %bitcast.5, bf16[3,8,128]{2,1,0:T(8,128)(2,1)} %bitcast.6, s32[8,128]{1,0:T(8,128)} %state_h.1, s32[8,128]{1,0:T(8,128)} %cell_h.1, ...), custom_call_target="tpu_custom_call" | custom-call | tf_op jit(solution)/shard_map/exchange/pallas_call | solution.py:358
  36.3 1.7 %store.1 = (f32[128,512]{1,0:T(8,128)}, f32[3,8,128]{2,1,0:T(8,128)}, f32[3,8,128]{2,1,0:T(8,128)}) custom-call(f32[6,8,128]{2,1,0:T(8,128)} %get-tuple-element.8.faces_h, f32[128,512]{1,0:T(8,128)} %get-tuple-element.9.flow_h), custom_call_target="tpu_custom_call" | custom-call | tf_op jit(solution)/shard_map/store/pallas_call | solution.py:408

commit v3 on v2

--- a/solution.py
+++ b/solution.py
@@ -13,6 +13,9 @@
 
 NP = 8
 NZ = 8
+FAR = (4, 3, 5, 2, 6, 1, 7, 0)
+COLUMN_ORDER = (4, 5, 3, 2, 6, 1, 7)
+HALF = NP * 16
 F32 = jnp.float32
 BF16 = jnp.bfloat16
 I32 = jnp.int32
@@ -50,7 +53,7 @@
 def exchange_kernel(
     pressure_h, prev_h, perm_h, uplus_h, uminus_h, state_h, cell_h, dest_h, target_h, source_h, mortar_h,
     faces_o, flow_o,
-    pres, prev, perm, mort, flow, proj, slots_t, owner, weight, zsend, zrecv, csend, crecv, xsend, xrecv,
+    pres, prev, perm, mort, flow, proj, slots_t, owner, zsend, zrecv, csend, crecv, xsend, xrecv,
     tsend, trecv, rsend, rrecv, row_send, row_recv, col_send, col_recv, node_p,
     uplus_r, uminus_r, state_r, cell_r, dest_r, target_r, source_s, by_patch,
     fsem, msem, lsem, zss, zrs, css, crs, xss, xrs, tss, trs, rss, rrs, hss, hrs, osem,
@@ -70,6 +73,13 @@
     seg_up, seg_down = {"seg": lax.rem(seg + 1, n_seg)}, {"seg": lax.rem(seg + n_seg - 1, n_seg)}
     dev_up, dev_down = {"dev": lax.rem(me + 1, n_dev)}, {"dev": lax.rem(me + n_dev - 1, n_dev)}
 
+    barrier = pltpu.get_barrier_semaphore()
+    neighbours = [column(lax.rem(pos + i, NP)) for i in COLUMN_ORDER]
+    neighbours += [row(lax.rem(z + i, NZ)) for i in FAR[:7]]
+    neighbours += [seg_up, seg_down, dev_up, dev_down]
+    for device in neighbours:
+        pl.semaphore_signal(barrier, inc=1, device_id=device, device_id_type=MESH)
+
     def fetch(pairs, sems):
         copies = [pltpu.make_async_copy(a, b, sems.at[i]) for i, (a, b) in enumerate(pairs)]
         for copy in copies:
@@ -86,19 +96,13 @@
         lsem,
     )
 
-    barrier = pltpu.get_barrier_semaphore()
-    for i in range(1, NP):
-        pl.semaphore_signal(barrier, inc=1, device_id=column(lax.rem(pos + i, NP)), device_id_type=MESH)
-    for i in range(1, NZ):
-        pl.semaphore_signal(barrier, inc=1, device_id=row(lax.rem(z + i, NZ)), device_id_type=MESH)
-    for device in (seg_up, seg_down, dev_up, dev_down):
-        pl.semaphore_signal(barrier, inc=1, device_id=device, device_id_type=MESH)
-
     for copy in first:
         copy.wait()
+    by_patch[...] = jnp.zeros_like(by_patch)
     for b in range(8):
         for c in range(3):
-            by_patch[b, c : c + 1, :] = uminus_r[c].astype(F32)[b : b + 1, :]
+            by_patch[0, b, c : c + 1, :] = uminus_r[c].astype(F32)[b : b + 1, :]
+            by_patch[1, b, 4 + c : 5 + c, :] = uminus_r[c].astype(F32)[b : b + 1, :]
 
     lane, sub = iota((64, 128), 1), iota((64, 128), 0)
     diagonal = lane == sub
@@ -111,42 +115,56 @@
     dest_row, dest = as_column(dest_r)
     _, target = as_column(target_r)
     rank = jnp.sum(jnp.where((dest_row == dest) & (lane < sub), 1, 0), axis=1, keepdims=True)
-    slot = ((dest & (NP - 1)) * NZ + (dest >> 3)) * CAP + rank
+    distance = ((dest >> 3) + NZ - z) & (NZ - 1)
+    turn = jnp.zeros((64, 1), I32)
+    for i in range(NZ):
+        turn = jnp.where(distance == FAR[i], i, turn)
+    slot = (turn >> 2) * HALF + (dest & (NP - 1)) * 16 + (turn & 3) * CAP + rank
     for h in range(2):
         slots_t[:, 128 * h : 128 * (h + 1)] = jnp.where(slot == lane + 128 * h, 1.0, 0.0).astype(BF16)
     for g in range(8):
         mcopies[g].wait()
-
-        def project(j, carry):
+        lines = [[], [], []]
+        for j in range(0, 8, 2):
             q = 8 * g + j
-            value = dot_nt(by_patch[source_s[q]].astype(BF16), mort[q])
+            left = (by_patch[0, source_s[q]] + by_patch[1, source_s[q + 1]]).astype(BF16)
+            value = dot_nt(left, mort[q : q + 2].reshape(256, 128))
             for c in range(3):
-                proj[pl.ds(q, 1), 128 * c : 128 * (c + 1)] = value[c : c + 1, :]
-            return carry
-
-        lax.fori_loop(0, 8, project, 0, unroll=True)
+                lines[c] += [value[c : c + 1, 0:128], value[4 + c : 5 + c, 128:256]]
+        for c in range(3):
+            proj[8 * g : 8 * (g + 1), 128 * c : 128 * (c + 1)] = jnp.concatenate(lines[c], axis=0)
     size = jnp.max(jnp.abs(proj[...]), axis=1, keepdims=True)
     power = jnp.floor(jnp.log2(jnp.maximum(size, 1e-30))) + 1.0
     whole = jnp.clip(jnp.round(proj[...] * jnp.exp2(15.0 - power)), -32767.0, 32767.0)
     label = target.astype(F32) + 8.0 * (power + 128.0)
     for p in range(NP):
-        code = jnp.sum(jnp.where(slot == (lane & 31) + 32 * p, label, 0.0), axis=0, keepdims=True)
-        csend[p] = jnp.broadcast_to(code, (8, 128))
+        for h in range(2):
+            spot = slot == (lane & 15) + (h * HALF + 16 * p)
+            csend[p, h : h + 1, :] = jnp.sum(jnp.where(spot, label, 0.0), axis=0, keepdims=True)
     high, low = split2(whole)
-    hit = slots_t[...]
-    zsend[...] = (dot_tn(hit, high) + dot_tn(hit, low)).astype(I32).astype(I16).reshape(NP, 32, 384)
-
-    pl.semaphore_wait(barrier, NP - 1 + NZ - 1 + 4)
-
-    zcopies, ccopies = [], []
-    for i in range(1, NP):
+
+    def place(h):
+        hit = slots_t[:, HALF * h : HALF * (h + 1)]
+        zsend[h] = (dot_tn(hit, high) + dot_tn(hit, low)).astype(I32).astype(I16).reshape(NP, 16, 384)
+
+    place(0)
+    pl.semaphore_wait(barrier, len(neighbours))
+
+    ccopies, zcopies = [], []
+    for i in COLUMN_ORDER:
         p = lax.rem(pos + i, NP)
         ccopies.append(remote(csend.at[p], crecv.at[pos], css.at[i], crs.at[pos], column(p)))
-        zcopies.append(remote(zsend.at[p], zrecv.at[pos], zss.at[i], zrs.at[pos], column(p)))
+        zcopies.append(remote(zsend.at[0, p], zrecv.at[0, pos], zss.at[0, i], zrs.at[0, pos], column(p)))
         ccopies[-1].start()
         zcopies[-1].start()
+    place(1)
+    for i in COLUMN_ORDER:
+        p = lax.rem(pos + i, NP)
+        zcopies.append(remote(zsend.at[1, p], zrecv.at[1, pos], zss.at[1, i], zrs.at[1, pos], column(p)))
+        zcopies[-1].start()
     crecv[pos] = csend[pos]
-    zrecv[pos] = zsend[pos]
+    for h in range(2):
+        zrecv[h, pos] = zsend[h, pos]
 
     for copy in lcopies:
         copy.wait()
@@ -192,29 +210,30 @@
 
     node_p[...] = lax.fori_loop(0, 16, look, jnp.zeros((8, 128), F32))
 
-    for i in range(1, NP):
+    for i in COLUMN_ORDER:
         p = lax.rem(pos + i, NP)
         remote(csend.at[p], crecv.at[p], css.at[i], crs.at[p], column(p)).wait_recv()
-        remote(zsend.at[p], zrecv.at[p], zss.at[i], zrs.at[p], column(p)).wait_recv()
+    lane32, sub32 = iota((32, 128), 1), iota((32, 128), 0)
+    in_turn = ((lane32 & 15) >> 2) == (sub32 >> 3)
+    codes = crecv[0]
+    for p in range(1, NP):
+        codes = jnp.where((iota((8, 128), 1) >> 4) == p, crecv[p], codes)
+    xcopies = []
     for h in range(2):
-        code = jnp.zeros((8, 128), F32)
-        for p in range(4):
-            code = jnp.where((iota((8, 128), 1) >> 5) == p, crecv[4 * h + p], code)
-        code = jnp.broadcast_to(code[0:1, :], (64, 128)).astype(I32)
+        code = jnp.broadcast_to(codes[h : h + 1, :], (32, 128)).astype(I32)
         scale = jnp.exp2((code >> 3).astype(F32) - (128.0 + 15.0))
-        match = ((code & 7) == (sub & 7)) & (((lane & 31) >> 2) == (sub >> 3))
-        owner[:, 128 * h : 128 * (h + 1)] = jnp.where(match, 1.0, 0.0).astype(BF16)
-        weight[:, 128 * h : 128 * (h + 1)] = jnp.where(match, scale, 0.0).astype(BF16)
-    high, low = split2(zrecv[...].reshape(256, 384).astype(I32).astype(F32))
-    weights = weight[...]
-    dense = dot_nn(weights, high) + dot_nn(weights, low)
-    xsend[...] = dense.reshape(NZ, 8, 384)
-    xcopies = []
-    for i in range(1, NZ):
-        zz = lax.rem(z + i, NZ)
-        xcopies.append(remote(xsend.at[zz], xrecv.at[z], xss.at[i], xrs.at[z], row(zz)))
-        xcopies[-1].start()
-    xrecv[z] = xsend[z]
+        match = ((code & 7) == (sub32 & 7)) & in_turn
+        owner[h] = jnp.where(match, 1.0, 0.0).astype(BF16)
+        weight = jnp.where(match, scale, 0.0).astype(BF16)
+        for i in COLUMN_ORDER:
+            p = lax.rem(pos + i, NP)
+            remote(zsend.at[h, p], zrecv.at[h, p], zss.at[h, i], zrs.at[h, p], column(p)).wait_recv()
+        high, low = split2(zrecv[h].reshape(HALF, 384).astype(I32).astype(F32))
+        xsend[4 * h : 4 * (h + 1)] = (dot_nn(weight, high) + dot_nn(weight, low)).reshape(4, 8, 384)
+        for i in range(4 * h, min(4 * h + 4, NZ - 1)):
+            there, back = row(lax.rem(z + FAR[i], NZ)), FAR.index((NZ - FAR[i]) % NZ)
+            xcopies.append(remote(xsend.at[i], xrecv.at[back], xss.at[i], xrs.at[back], there))
+            xcopies[-1].start()
 
     for i in range(4):
         hcopies[i].wait_recv()
@@ -266,11 +285,9 @@
     flow_copy = pltpu.make_async_copy(flow, flow_o, osem.at[0])
     flow_copy.start()
 
-    for i in range(1, NZ):
-        zz = lax.rem(z + i, NZ)
-        remote(xsend.at[zz], xrecv.at[zz], xss.at[i], xrs.at[zz], row(zz)).wait_recv()
-    mortar_sum = xrecv[0]
-    for i in range(1, NZ):
+    mortar_sum = xsend[NZ - 1]
+    for i in range(NZ - 2, -1, -1):
+        remote(xsend.at[i], xrecv.at[i], xss.at[i], xrs.at[i], row(lax.rem(z + FAR[i], NZ))).wait_recv()
         mortar_sum = mortar_sum + xrecv[i]
     jump = [uplus_r[c] - mortar_sum[:, 128 * c : 128 * (c + 1)] for c in range(3)]
     normal_part = PENALTY * jump[0]
@@ -282,46 +299,47 @@
     traction = [
         jnp.where(state == 0, PENALTY * jump[c], jnp.where(state == 1, sliding[c], 0.0)) for c in range(3)
     ]
+    tsend[...] = jnp.concatenate(traction + [jnp.zeros((8, 128), F32)], axis=0).astype(BF16)
+    tcopies = []
+    for i in range(NZ - 1):
+        there, back = row(lax.rem(z + FAR[i], NZ)), FAR.index((NZ - FAR[i]) % NZ)
+        tcopies.append(remote(tsend, trecv.at[back], tss.at[i], trs.at[back], there))
+        tcopies[-1].start()
+    trecv[NZ - 1] = tsend[...]
     for c in range(3):
         faces_o[c] = traction[c]
-    tsend[...] = jnp.concatenate(traction + [jnp.zeros((8, 128), F32)], axis=0).astype(BF16)
-    tcopies = []
-    for i in range(1, NZ):
-        zz = lax.rem(z + i, NZ)
-        tcopies.append(remote(tsend, trecv.at[z], tss.at[i], trs.at[z], row(zz)))
-        tcopies[-1].start()
-    trecv[z] = tsend[...]
-    for i in range(1, NZ):
-        zz = lax.rem(z + i, NZ)
-        remote(tsend, trecv.at[zz], tss.at[i], trs.at[zz], row(zz)).wait_recv()
-
-    got = trecv[...].astype(F32)
-    table = jnp.concatenate([got[:, 8 * c : 8 * (c + 1), :].reshape(64, 128) for c in range(3)], axis=1)
-    rsend[...] = dot_tn(owner[...], table.astype(BF16)).astype(BF16).reshape(NP, 32, 384)
+
     rcopies = []
-    for i in range(1, NP):
-        p = lax.rem(pos + i, NP)
-        rcopies.append(remote(rsend.at[p], rrecv.at[pos], rss.at[i], rrs.at[pos], column(p)))
-        rcopies[-1].start()
-    rrecv[pos] = rsend[pos]
-    for i in range(1, NP):
-        p = lax.rem(pos + i, NP)
-        remote(rsend.at[p], rrecv.at[p], rss.at[i], rrs.at[p], column(p)).wait_recv()
-    proj[...] = dot_nn(slots_t[...], rrecv[...].reshape(256, 384))
+    for h in (1, 0):
+        for i in range(min(4 * h + 3, NZ - 2), 4 * h - 1, -1):
+            remote(tsend, trecv.at[i], tss.at[i], trs.at[i], row(lax.rem(z + FAR[i], NZ))).wait_recv()
+        got = trecv[4 * h : 4 * (h + 1)].astype(F32)
+        table = jnp.concatenate([got[:, 8 * c : 8 * (c + 1), :].reshape(32, 128) for c in range(3)], axis=1)
+        rsend[h] = dot_tn(owner[h], table.astype(BF16)).astype(BF16).reshape(NP, 16, 384)
+        for i in COLUMN_ORDER:
+            p = lax.rem(pos + i, NP)
+            rcopies.append(remote(rsend.at[h, p], rrecv.at[h, pos], rss.at[h, i], rrs.at[h, pos], column(p)))
+            rcopies[-1].start()
+        rrecv[h, pos] = rsend[h, pos]
+    replies = jnp.zeros((64, 384), F32)
+    for h in (1, 0):
+        for i in COLUMN_ORDER:
+            p = lax.rem(pos + i, NP)
+            remote(rsend.at[h, p], rrecv.at[h, p], rss.at[h, i], rrs.at[h, p], column(p)).wait_recv()
+        replies = replies + dot_nn(slots_t[:, HALF * h : HALF * (h + 1)], rrecv[h].reshape(HALF, 384))
 
     patch = iota((8, 128), 0)
     total = jnp.zeros((32, 128), F32)
-    for g in range(8):
-        values = proj[8 * g : 8 * (g + 1), :]
-        for j in range(8):
-            q = 8 * g + j
-            mine = patch == source_s[q]
+    for q in range(0, 64, 2):
+        left = []
+        for k in range(2):
+            mine = patch == source_s[q + k]
             rows = [
-                jnp.where(mine, jnp.broadcast_to(values[j : j + 1, 128 * c : 128 * (c + 1)], (8, 128)), 0.0)
+                jnp.where(mine, jnp.broadcast_to(replies[q + k : q + k + 1, 128 * c : 128 * (c + 1)], (8, 128)), 0.0)
                 for c in range(3)
             ]
-            left = jnp.concatenate(rows + [jnp.zeros((8, 128), F32)], axis=0).astype(BF16)
-            total = total + dot_nn(left, mort[q])
+            left.append(jnp.concatenate(rows + [jnp.zeros((8, 128), F32)], axis=0).astype(BF16))
+        total = total + dot_nn(jnp.concatenate(left, axis=1), mort[q : q + 2].reshape(256, 128))
     for c in range(3):
         faces_o[3 + c] = -total[8 * c : 8 * (c + 1), :]
 
@@ -368,18 +386,17 @@
             pltpu.VMEM((128, 512), F32),
             pltpu.VMEM((64, 384), F32),
             pltpu.VMEM((64, 256), BF16),
-            pltpu.VMEM((64, 256), BF16),
-            pltpu.VMEM((64, 256), BF16),
-            pltpu.VMEM((NP, 32, 384), I16),
-            pltpu.VMEM((NP, 32, 384), I16),
+            pltpu.VMEM((2, 32, HALF), BF16),
+            pltpu.VMEM((2, NP, 16, 384), I16),
+            pltpu.VMEM((2, NP, 16, 384), I16),
             pltpu.VMEM((NP, 8, 128), F32),
             pltpu.VMEM((NP, 8, 128), F32),
             pltpu.VMEM((NZ, 8, 384), F32),
             pltpu.VMEM((NZ, 8, 384), F32),
             pltpu.VMEM((32, 128), BF16),
             pltpu.VMEM((NZ, 32, 128), BF16),
-            pltpu.VMEM((NP, 32, 384), BF16),
-            pltpu.VMEM((NP, 32, 384), BF16),
+            pltpu.VMEM((2, NP, 16, 384), BF16),
+            pltpu.VMEM((2, NP, 16, 384), BF16),
             pltpu.VMEM((2, 8, 128), F32),
             pltpu.VMEM((2, 8, 128), F32),
             pltpu.VMEM((2, 8, 128), F32),
@@ -392,10 +409,10 @@
             pltpu.VMEM((64,), I32),
             pltpu.VMEM((64,), I32),
             pltpu.SMEM((64,), I32),
-            pltpu.VMEM((8, 8, 128), F32),
+            pltpu.VMEM((2, 8, 8, 128), F32),
             dma((4,)), dma((8,)), dma((6,)),
-            dma((8,)), dma((8,)), dma((8,)), dma((8,)), dma((8,)), dma((8,)),
-            dma((8,)), dma((8,)), dma((8,)), dma((8,)), dma((4,)), dma((4,)), dma((1,)),
+            dma((2, 8)), dma((2, 8)), dma((8,)), dma((8,)), dma((8,)), dma((8,)),
+            dma((8,)), dma((8,)), dma((2, 8)), dma((2, 8)), dma((4,)), dma((4,)), dma((1,)),
         ],
         compiler_params=pltpu.CompilerParams(
             collective_id=0, has_side_effects=True, vmem_limit_bytes=60 * 1024 * 1024

time: 38.2 us -> 35.6 us (0.932)
  Pallas kernels: 37.4 us -> 34.8 us
    pallas_call x1, Pallas kernels: 35.7 us -> 33.1 us  [on_device(): pl.pallas_call(exchange_kernel, out_shape=(shape((6, 8, 128), F32), shape...]
where the time goes in v3:
time: 35.6 us; the launch traced here: 35.5 us
  Pallas kernels  34.8 us (98%)
  between operations  0.64 us (2%)
    pallas_call x1, Pallas kernels, on_device(): pl.pallas_call(exchange_kernel, out_shape=(shape((6, 8, 128), F32), shape...  33.1 us
    pallas_call x1, Pallas kernels, on_device(): pl.pallas_call(store_kernel, out_shape=(shape((128, 512), F32), shape((3,...  1.71 us

profile of v3, /device:TPU:1, one launch (start us, length us, event | category | flops | bytes accessed | tf_op | source)
XLA Modules:
  0.0 35.5 jit_solution(668522481108316948)
XLA Ops:
  0.6 33.1 %exchange.1 = (f32[6,8,128]{2,1,0:T(8,128)}, f32[128,512]{1,0:T(8,128)}) custom-call(f32[128,512]{1,0:T(8,128)} %pressure_h.1, f32[128,512]{1,0:T(8,128)} %prev_h.1, f32[128,512]{1,0:T(8,128)} %perm_h.1, f32[3,8,128]{2,1,0:T(8,128)} %bitcast.5, bf16[3,8,128]{2,1,0:T(8,128)(2,1)} %bitcast.6, s32[8,128]{1,0:T(8,128)} %state_h.1, s32[8,128]{1,0:T(8,128)} %cell_h.1, ...), custom_call_target="tpu_custom_call" | custom-call | tf_op jit(solution)/shard_map/exchange/pallas_call | solution.py:376
  33.8 1.7 %store.1 = (f32[128,512]{1,0:T(8,128)}, f32[3,8,128]{2,1,0:T(8,128)}, f32[3,8,128]{2,1,0:T(8,128)}) custom-call(f32[6,8,128]{2,1,0:T(8,128)} %get-tuple-element.8.faces_h, f32[128,512]{1,0:T(8,128)} %get-tuple-element.9.flow_h), custom_call_target="tpu_custom_call" | custom-call | tf_op jit(solution)/shard_map/store/pallas_call | solution.py:425

commit v4 on v3

--- a/solution.py
+++ b/solution.py
@@ -53,10 +53,10 @@
 def exchange_kernel(
     pressure_h, prev_h, perm_h, uplus_h, uminus_h, state_h, cell_h, dest_h, target_h, source_h, mortar_h,
     faces_o, flow_o,
-    pres, prev, perm, mort, flow, proj, slots_t, owner, zsend, zrecv, csend, crecv, xsend, xrecv,
+    pres, prev, perm, mort, proj, slots_t, owner, zsend, zrecv, csend, crecv, xsend, xrecv,
     tsend, trecv, rsend, rrecv, row_send, row_recv, col_send, col_recv, node_p,
     uplus_r, uminus_r, state_r, cell_r, dest_r, target_r, source_s, by_patch,
-    fsem, msem, lsem, zss, zrs, css, crs, xss, xrs, tss, trs, rss, rrs, hss, hrs, osem,
+    fsem, msem, lsem, zss, zrs, css, crs, xss, xrs, tss, trs, rss, rrs, hss, hrs,
 ):
     seg = lax.axis_index("seg")
     me = lax.axis_index("dev")
@@ -281,9 +281,7 @@
         total = COMPRESS * (p - prev[rows, :])
         total = total + edge_term(p, k, pd, kd) + edge_term(p, k, pu, ku)
         total = total + edge_term(p, k, pright, kright) + edge_term(p, k, pleft, kleft)
-        flow[rows, :] = total
-    flow_copy = pltpu.make_async_copy(flow, flow_o, osem.at[0])
-    flow_copy.start()
+        flow_o[rows, :] = total
 
     mortar_sum = xsend[NZ - 1]
     for i in range(NZ - 2, -1, -1):
@@ -321,6 +319,8 @@
             rcopies.append(remote(rsend.at[h, p], rrecv.at[h, pos], rss.at[h, i], rrs.at[h, pos], column(p)))
             rcopies[-1].start()
         rrecv[h, pos] = rsend[h, pos]
+    for copy in ccopies + zcopies + hcopies + xcopies + tcopies + rcopies:
+        copy.wait_send()
     replies = jnp.zeros((64, 384), F32)
     for h in (1, 0):
         for i in COLUMN_ORDER:
@@ -343,25 +343,15 @@
     for c in range(3):
         faces_o[3 + c] = -total[8 * c : 8 * (c + 1), :]
 
-    for copy in ccopies + zcopies + hcopies + xcopies + tcopies + rcopies:
-        copy.wait_send()
-    flow_copy.wait()
-
-
-def store_kernel(faces_h, flow_h, flow_o, traction_o, force_o, faces, flow, lsem, osem):
-    loads = [pltpu.make_async_copy(faces_h, faces, lsem.at[0]), pltpu.make_async_copy(flow_h, flow, lsem.at[1])]
+
+def store_kernel(faces, flow, flow_o, traction_o, force_o, osem):
     stores = [
         pltpu.make_async_copy(faces.at[pl.ds(0, 3)], traction_o, osem.at[0]),
         pltpu.make_async_copy(faces.at[pl.ds(3, 3)], force_o, osem.at[1]),
         pltpu.make_async_copy(flow, flow_o, osem.at[2]),
     ]
-    for copy in loads:
+    for copy in stores:
         copy.start()
-    loads[0].wait()
-    stores[0].start()
-    stores[1].start()
-    loads[1].wait()
-    stores[2].start()
     for copy in stores:
         copy.wait()
 
@@ -377,13 +367,12 @@
         exchange_kernel,
         out_shape=(shape((6, 8, 128), F32), shape((128, 512), F32)),
         in_specs=[hbm] * 11,
-        out_specs=(vmem, hbm),
+        out_specs=(vmem, vmem),
         scratch_shapes=[
             pltpu.VMEM((128, 512), F32),
             pltpu.VMEM((128, 512), F32),
             pltpu.VMEM((128, 512), F32),
             pltpu.VMEM((64, 128, 128), BF16),
-            pltpu.VMEM((128, 512), F32),
             pltpu.VMEM((64, 384), F32),
             pltpu.VMEM((64, 256), BF16),
             pltpu.VMEM((2, 32, HALF), BF16),
@@ -412,23 +401,28 @@
             pltpu.VMEM((2, 8, 8, 128), F32),
             dma((4,)), dma((8,)), dma((6,)),
             dma((2, 8)), dma((2, 8)), dma((8,)), dma((8,)), dma((8,)), dma((8,)),
-            dma((8,)), dma((8,)), dma((2, 8)), dma((2, 8)), dma((4,)), dma((4,)), dma((1,)),
+            dma((8,)), dma((8,)), dma((2, 8)), dma((2, 8)), dma((4,)), dma((4,)),
         ],
         compiler_params=pltpu.CompilerParams(
-            collective_id=0, has_side_effects=True, vmem_limit_bytes=60 * 1024 * 1024
+            collective_id=0, has_side_effects=True, vmem_limit_bytes=48 * 1024 * 1024
         ),
         name="exchange",
     )(
-        pressure, pressure_prev, permeability, u_plus.transpose(1, 0, 2), u_minus.transpose(1, 0, 2),
-        node_state, node_cell, pair_dest.reshape(64), pair_target, pair_source, mortar,
+        *(
+            pltpu.with_memory_space_constraint(a, pltpu.HBM)
+            for a in (
+                pressure, pressure_prev, permeability, u_plus.transpose(1, 0, 2), u_minus.transpose(1, 0, 2),
+                node_state, node_cell, pair_dest.reshape(64), pair_target, pair_source, mortar,
+            )
+        )
     )
     flow, traction, force = pl.pallas_call(
         store_kernel,
         out_shape=(shape((128, 512), F32), shape((3, 8, 128), F32), shape((3, 8, 128), F32)),
-        in_specs=[hbm, hbm],
+        in_specs=[vmem, vmem],
         out_specs=(hbm, hbm, hbm),
-        scratch_shapes=[pltpu.VMEM((6, 8, 128), F32), pltpu.VMEM((128, 512), F32), dma((2,)), dma((3,))],
-        compiler_params=pltpu.CompilerParams(vmem_limit_bytes=60 * 1024 * 1024),
+        scratch_shapes=[dma((3,))],
+        compiler_params=pltpu.CompilerParams(vmem_limit_bytes=48 * 1024 * 1024),
         name="store",
     )(faces, flow)
     return flow, traction.transpose(1, 0, 2), force.transpose(1, 0, 2)

time: 35.6 us -> 34 us (0.955)
  Pallas kernels: 34.8 us -> 33.2 us
    pallas_call x1, Pallas kernels: 1.71 us -> 0.74 us  [on_device(): pl.pallas_call(store_kernel, out_shape=(shape((128, 512), F32), shape((3,...]
    pallas_call x1, Pallas kernels: 33.1 us -> 32.4 us  [on_device(): pl.pallas_call(exchange_kernel, out_shape=(shape((6, 8, 128), F32), shape...]
where the time goes in v4:
time: 34 us; the launch traced here: 33.8 us
  Pallas kernels  33.2 us (98%)
  between operations  0.64 us (2%)
    pallas_call x1, Pallas kernels, on_device(): pl.pallas_call(exchange_kernel, out_shape=(shape((6, 8, 128), F32), shape...  32.4 us
    pallas_call x1, Pallas kernels, on_device(): pl.pallas_call(store_kernel, out_shape=(shape((128, 512), F32), shape((3,...  0.74 us

profile of v4, /device:TPU:1, one launch (start us, length us, event | category | flops | bytes accessed | tf_op | source)
XLA Modules:
  0.0 33.8 jit_solution(14750263942451687773)
XLA Ops:
  0.6 32.4 %exchange.1 = (f32[6,8,128]{2,1,0:T(8,128)S(1)}, f32[128,512]{1,0:T(8,128)S(1)}) custom-call(f32[128,512]{1,0:T(8,128)} %pressure_h.1, f32[128,512]{1,0:T(8,128)} %prev_h.1, f32[128,512]{1,0:T(8,128)} %perm_h.1, f32[3,8,128]{2,1,0:T(8,128)} %bitcast.5, bf16[3,8,128]{2,1,0:T(8,128)(2,1)} %bitcast.6, s32[8,128]{1,0:T(8,128)} %state_h.1, s32[8,128]{1,0:T(8,128)} %cell_h.1, ...), custom_call_target="tpu_custom_call" | custom-call | tf_op jit(solution)/shard_map/exchange/pallas_call | solution.py:366
  33.1 0.7 %store.1 = (f32[128,512]{1,0:T(8,128)}, f32[3,8,128]{2,1,0:T(8,128)}, f32[3,8,128]{2,1,0:T(8,128)}) custom-call(f32[6,8,128]{2,1,0:T(8,128)S(1)} %get-tuple-element.8.faces, f32[128,512]{1,0:T(8,128)S(1)} %get-tuple-element.9.flow), custom_call_target="tpu_custom_call" | custom-call | tf_op jit(solution)/shard_map/store/pallas_call | solution.py:419

commit v5 on v4

--- a/solution.py
+++ b/solution.py
@@ -74,8 +74,8 @@
     dev_up, dev_down = {"dev": lax.rem(me + 1, n_dev)}, {"dev": lax.rem(me + n_dev - 1, n_dev)}
 
     barrier = pltpu.get_barrier_semaphore()
-    neighbours = [column(lax.rem(pos + i, NP)) for i in COLUMN_ORDER]
-    neighbours += [row(lax.rem(z + i, NZ)) for i in FAR[:7]]
+    neighbours = [row(lax.rem(z + i, NZ)) for i in FAR[:7]]
+    neighbours += [column(lax.rem(pos + i, NP)) for i in COLUMN_ORDER]
     neighbours += [seg_up, seg_down, dev_up, dev_down]
     for device in neighbours:
         pl.semaphore_signal(barrier, inc=1, device_id=device, device_id_type=MESH)
@@ -88,14 +88,6 @@
 
     first = fetch(((dest_h, dest_r), (target_h, target_r), (source_h, source_s), (uminus_h, uminus_r)), fsem)
     mcopies = fetch([(mortar_h.at[pl.ds(8 * g, 8)], mort.at[pl.ds(8 * g, 8)]) for g in range(8)], msem)
-    lcopies = fetch(
-        (
-            (pressure_h, pres), (cell_h, cell_r), (perm_h, perm), (prev_h, prev),
-            (uplus_h, uplus_r), (state_h, state_r),
-        ),
-        lsem,
-    )
-
     for copy in first:
         copy.wait()
     by_patch[...] = jnp.zeros_like(by_patch)
@@ -122,8 +114,17 @@
     slot = (turn >> 2) * HALF + (dest & (NP - 1)) * 16 + (turn & 3) * CAP + rank
     for h in range(2):
         slots_t[:, 128 * h : 128 * (h + 1)] = jnp.where(slot == lane + 128 * h, 1.0, 0.0).astype(BF16)
+    for copy in mcopies:
+        copy.wait()
+    lcopies = fetch(
+        (
+            (pressure_h, pres), (cell_h, cell_r), (perm_h, perm), (prev_h, prev),
+            (uplus_h, uplus_r), (state_h, state_r),
+        ),
+        lsem,
+    )
+
     for g in range(8):
-        mcopies[g].wait()
         lines = [[], [], []]
         for j in range(0, 8, 2):
             q = 8 * g + j
@@ -153,7 +154,7 @@
     ccopies, zcopies = [], []
     for i in COLUMN_ORDER:
         p = lax.rem(pos + i, NP)
-        ccopies.append(remote(csend.at[p], crecv.at[pos], css.at[i], crs.at[pos], column(p)))
+        ccopies.append(remote(csend.at[p, pl.ds(0, 2)], crecv.at[pos, pl.ds(0, 2)], css.at[i], crs.at[pos], column(p)))
         zcopies.append(remote(zsend.at[0, p], zrecv.at[0, pos], zss.at[0, i], zrs.at[0, pos], column(p)))
         ccopies[-1].start()
         zcopies[-1].start()
@@ -212,7 +213,7 @@
 
     for i in COLUMN_ORDER:
         p = lax.rem(pos + i, NP)
-        remote(csend.at[p], crecv.at[p], css.at[i], crs.at[p], column(p)).wait_recv()
+        remote(csend.at[p, pl.ds(0, 2)], crecv.at[p, pl.ds(0, 2)], css.at[i], crs.at[p], column(p)).wait_recv()
     lane32, sub32 = iota((32, 128), 1), iota((32, 128), 0)
     in_turn = ((lane32 & 15) >> 2) == (sub32 >> 3)
     codes = crecv[0]

time: 34 us -> 33.5 us (0.985)
  Pallas kernels: 33.2 us -> 32.7 us
    pallas_call x1, Pallas kernels: 32.4 us -> 32 us  [on_device(): pl.pallas_call(exchange_kernel, out_shape=(shape((6, 8, 128), F32), shape...]
where the time goes in v5:
time: 33.5 us; the launch traced here: 33.4 us
  Pallas kernels  32.7 us (98%)
  between operations  0.64 us (2%)
    pallas_call x1, Pallas kernels, on_device(): pl.pallas_call(exchange_kernel, out_shape=(shape((6, 8, 128), F32), shape...  32 us
    pallas_call x1, Pallas kernels, on_device(): pl.pallas_call(store_kernel, out_shape=(shape((128, 512), F32), shape((3,...  0.74 us

profile of v5, /device:TPU:1, one launch (start us, length us, event | category | flops | bytes accessed | tf_op | source)
XLA Modules:
  0.0 33.4 jit_solution(7583212808410072623)
XLA Ops:
  0.6 32.0 %exchange.1 = (f32[6,8,128]{2,1,0:T(8,128)S(1)}, f32[128,512]{1,0:T(8,128)S(1)}) custom-call(f32[128,512]{1,0:T(8,128)} %pressure_h.1, f32[128,512]{1,0:T(8,128)} %prev_h.1, f32[128,512]{1,0:T(8,128)} %perm_h.1, f32[3,8,128]{2,1,0:T(8,128)} %bitcast.5, bf16[3,8,128]{2,1,0:T(8,128)(2,1)} %bitcast.6, s32[8,128]{1,0:T(8,128)} %state_h.1, s32[8,128]{1,0:T(8,128)} %cell_h.1, ...), custom_call_target="tpu_custom_call" | custom-call | tf_op jit(solution)/shard_map/exchange/pallas_call | solution.py:367
  32.7 0.7 %store.1 = (f32[128,512]{1,0:T(8,128)}, f32[3,8,128]{2,1,0:T(8,128)}, f32[3,8,128]{2,1,0:T(8,128)}) custom-call(f32[6,8,128]{2,1,0:T(8,128)S(1)} %get-tuple-element.8.faces, f32[128,512]{1,0:T(8,128)S(1)} %get-tuple-element.9.flow), custom_call_target="tpu_custom_call" | custom-call | tf_op jit(solution)/shard_map/store/pallas_call | solution.py:420

commit v6 on v5

--- a/solution.py
+++ b/solution.py
@@ -230,7 +230,13 @@
             p = lax.rem(pos + i, NP)
             remote(zsend.at[h, p], zrecv.at[h, p], zss.at[h, i], zrs.at[h, p], column(p)).wait_recv()
         high, low = split2(zrecv[h].reshape(HALF, 384).astype(I32).astype(F32))
-        xsend[4 * h : 4 * (h + 1)] = (dot_nn(weight, high) + dot_nn(weight, low)).reshape(4, 8, 384)
+        dense = dot_nn(weight, high) + dot_nn(weight, low)
+        size = jnp.max(jnp.abs(dense), axis=1, keepdims=True)
+        power = jnp.floor(jnp.log2(jnp.maximum(size, 1e-30))) + 1.0
+        whole = jnp.clip(jnp.round(dense * jnp.exp2(15.0 - power)), -32767.0, 32767.0)
+        blocks = [whole[:, 128 * c : 128 * (c + 1)].reshape(4, 8, 128) for c in range(3)]
+        blocks.append(jnp.broadcast_to(power, (32, 128)).reshape(4, 8, 128))
+        xsend[4 * h : 4 * (h + 1)] = jnp.concatenate(blocks, axis=1).astype(I32).astype(I16)
         for i in range(4 * h, min(4 * h + 4, NZ - 1)):
             there, back = row(lax.rem(z + FAR[i], NZ)), FAR.index((NZ - FAR[i]) % NZ)
             xcopies.append(remote(xsend.at[i], xrecv.at[back], xss.at[i], xrs.at[back], there))
@@ -284,11 +290,14 @@
         total = total + edge_term(p, k, pright, kright) + edge_term(p, k, pleft, kleft)
         flow_o[rows, :] = total
 
-    mortar_sum = xsend[NZ - 1]
-    for i in range(NZ - 2, -1, -1):
-        remote(xsend.at[i], xrecv.at[i], xss.at[i], xrs.at[i], row(lax.rem(z + FAR[i], NZ))).wait_recv()
-        mortar_sum = mortar_sum + xrecv[i]
-    jump = [uplus_r[c] - mortar_sum[:, 128 * c : 128 * (c + 1)] for c in range(3)]
+    mortar_sum = [jnp.zeros((8, 128), F32) for c in range(3)]
+    for i in range(NZ - 1, -1, -1):
+        if i < NZ - 1:
+            remote(xsend.at[i], xrecv.at[i], xss.at[i], xrs.at[i], row(lax.rem(z + FAR[i], NZ))).wait_recv()
+        got = (xsend[i] if i == NZ - 1 else xrecv[i]).astype(I32).astype(F32)
+        scale = jnp.exp2(got[24:32] - 15.0)
+        mortar_sum = [mortar_sum[c] + got[8 * c : 8 * (c + 1)] * scale for c in range(3)]
+    jump = [uplus_r[c] - mortar_sum[c] for c in range(3)]
     normal_part = PENALTY * jump[0]
     stress = CONFINING - node_p[...] - normal_part
     softplus = jnp.maximum(stress, 0.0) + jnp.log1p(jnp.exp(-jnp.abs(stress)))
@@ -381,8 +390,8 @@
             pltpu.VMEM((2, NP, 16, 384), I16),
             pltpu.VMEM((NP, 8, 128), F32),
             pltpu.VMEM((NP, 8, 128), F32),
-            pltpu.VMEM((NZ, 8, 384), F32),
-            pltpu.VMEM((NZ, 8, 384), F32),
+            pltpu.VMEM((NZ, 32, 128), I16),
+            pltpu.VMEM((NZ, 32, 128), I16),
             pltpu.VMEM((32, 128), BF16),
             pltpu.VMEM((NZ, 32, 128), BF16),
             pltpu.VMEM((2, NP, 16, 384), BF16),

time: 33.5 us -> 33.3 us (level)
  no operation moved by 1% of the time
where the time goes in v6:
time: 33.3 us; the launch traced here: 33.1 us
  Pallas kernels  32.5 us (98%)
  between operations  0.64 us (2%)
    pallas_call x1, Pallas kernels, on_device(): pl.pallas_call(exchange_kernel, out_shape=(shape((6, 8, 128), F32), shape...  31.7 us
    pallas_call x1, Pallas kernels, on_device(): pl.pallas_call(store_kernel, out_shape=(shape((128, 512), F32), shape((3,...  0.74 us

profile of v6, /device:TPU:1, one launch (start us, length us, event | category | flops | bytes accessed | tf_op | source)
XLA Modules:
  0.0 33.1 jit_solution(4221955245251008188)
XLA Ops:
  0.6 31.7 %exchange.1 = (f32[6,8,128]{2,1,0:T(8,128)S(1)}, f32[128,512]{1,0:T(8,128)S(1)}) custom-call(f32[128,512]{1,0:T(8,128)} %pressure_h.1, f32[128,512]{1,0:T(8,128)} %prev_h.1, f32[128,512]{1,0:T(8,128)} %perm_h.1, f32[3,8,128]{2,1,0:T(8,128)} %bitcast.5, bf16[3,8,128]{2,1,0:T(8,128)(2,1)} %bitcast.6, s32[8,128]{1,0:T(8,128)} %state_h.1, s32[8,128]{1,0:T(8,128)} %cell_h.1, ...), custom_call_target="tpu_custom_call" | custom-call | tf_op jit(solution)/shard_map/exchange/pallas_call | solution.py:376
  32.4 0.7 %store.1 = (f32[128,512]{1,0:T(8,128)}, f32[3,8,128]{2,1,0:T(8,128)}, f32[3,8,128]{2,1,0:T(8,128)}) custom-call(f32[6,8,128]{2,1,0:T(8,128)S(1)} %get-tuple-element.8.faces, f32[128,512]{1,0:T(8,128)S(1)} %get-tuple-element.9.flow), custom_call_target="tpu_custom_call" | custom-call | tf_op jit(solution)/shard_map/store/pallas_call | solution.py:429
